TPU v7x, 128 devices: a whole 4x4x4 slice. The times are simulated.
128 devices in a mesh: shot: 4 (over x_lo, core), aper: 32 (over z, y, x_hi).
Axes of the slice: x: 4 (x_hi: 2, x_lo: 2; x = x_hi * 2 + x_lo), y: 4, z: 4, core: 2. Of those that a mesh axis runs over, the one named last changes fastest.
Arguments:
- velocity: float32 [512, 32, 256], P(('shot', 'aper')), may hold values from 0.15 to 0.32
- thomsen_epsilon: float32 [512, 32, 256], P(('shot', 'aper')), may hold values from 0.12 to 0.3
- thomsen_delta: float32 [512, 32, 256], P(('shot', 'aper')), may hold values from -0.1 to 0.1
- tilt_angle: float32 [512, 32, 256], P(('shot', 'aper')), may hold values from -1 to 1
- fwd_now: float32 [4, 2, 128, 32, 256], P('shot', None, 'aper'), may hold values from -6 to 6
- fwd_before: float32 [4, 2, 128, 32, 256], P('shot', None, 'aper'), may hold values from -6 to 6
- adj_now: float32 [4, 2, 128, 32, 256], P('shot', None, 'aper'), may hold values from -6 to 6
- adj_before: float32 [4, 2, 128, 32, 256], P('shot', None, 'aper'), may hold values from -6 to 6
- wavelet: float32 [4, 4], replicated, may hold values from -12 to 12
- traces: float32 [4, 4, 256], replicated, may hold values from -10 to 10
- offsets: int32 [4], replicated, may hold values from 0 to 96, as said below
- source_cell: int32 [4, 3], replicated, may hold values from 0 to 255, as said below
- receiver_cell: int32 [4, 256, 3], replicated, may hold values from 0 to 127, as said below
Outputs:
- image_sum: float32 [512, 32, 256], P(('shot', 'aper'))
Inputs may be any that keep to these rules, and one draw needn't show every extreme that they name: `offsets`: model tiles are 4 cells long; in every draw one group has offset 0, one has (3) * 32, and one leaves the remainder 32 - 1 modulo 32. `source_cell`: first index below 128, second below 32, third below 256. `receiver_cell`: first index below 128, second below 32, third from 2 to 5; cells may coincide.
All inputs are finite; a program needn't handle non-finite values.
Results may differ from a plain program's by a relative error of at most 0.00002.
Values sent between devices are 32-bit elements; how exact they have to be, the bound alone decides.
No kernel may reach another device: no remote copies, remote signals or barrier semaphores. Data moves between devices by JAX's collectives and lax.ppermute only.
A program may use at most 64 MiB of HBM per device.

v0:
```python
import jax
import jax.numpy as jnp
from jax import lax
from jax.experimental import pallas as pl
from jax.experimental.pallas import tpu as pltpu
from jax.sharding import PartitionSpec as P

second_coef = (-205.0 / 72.0, 8.0 / 5.0, -1.0 / 5.0, 8.0 / 315.0, -1.0 / 560.0)
first_coef = (4.0 / 5.0, -1.0 / 5.0, 4.0 / 105.0, -1.0 / 280.0)

AXES = ("shot", "aper")
STEPS = 4
TX = 4
AY = 32
AZ = 256
HALF = 128
HALF_Y = AY // 2
F32 = jnp.float32
VMEM = pl.BlockSpec(memory_space=pltpu.VMEM)
SMEM = pl.BlockSpec(memory_space=pltpu.SMEM)


def device(x, core, y, z):
    return ((x % 2) * 2 + core) * 32 + ((z % 4) * 4 + y % 4) * 2 + x // 2


def everyone():
    return [(x, c, y, z) for x in range(4) for c in range(2) for y in range(4) for z in range(4)]


def flipped(y, z):
    return 3 - y if z % 2 else y


def on_path(j):
    j = j % 16
    return flipped(j % 4, j // 4), j // 4


def path_place(y, z):
    return 4 * z + flipped(y, z)


def pairs_of(rule):
    pairs = [(device(*d), device(*rule(*d))) for d in everyone()]
    assert sorted(t for _, t in pairs) == list(range(128))
    assert all(s != t for s, t in pairs)
    return pairs


def send(value, pairs):
    return lax.ppermute(value, AXES, pairs)


def other_core():
    return pairs_of(lambda x, c, y, z: (x, 1 - c, y, z))


def along_path(by):
    def rule(x, c, y, z):
        return (x, c) + on_path(path_place(y, z) + by)

    return pairs_of(rule)


def state_first():
    def rule(x, c, y, z):
        hi = x // 2
        t = {(0, 0): (0, 1), (0, 1): (1, 1), (1, 0): (0, 0), (1, 1): (1, 0)}[(hi, c)]
        return (2 * t[0] + x % 2, t[1], flipped(y, z), z)

    return pairs_of(rule)


def state_second():
    def rule(x, c, y, z):
        hi = x // 2
        if hi == c:
            return (x, c, 3 - y, z)
        return (2 * (1 - hi) + x % 2, 1 - c, flipped(y, z), z)

    return pairs_of(rule)


def across(by):
    def rule(x, c, y, z):
        if by == 0:
            return (x, c, 3 - y, z)
        return ((x + by) % 4, c, flipped(y, z), z)

    return pairs_of(rule)


def rolled(by_low, by_high):
    def rule(x, c, y, z):
        j = (4 * z + y + (by_high if x // 2 else by_low)) % 16
        return (x, c, j % 4, j // 4)

    return pairs_of(rule)


def z_plus(pair, d, lane):
    a, b = pair
    ra, rb = pltpu.roll(a, HALF - d, 1), pltpu.roll(b, HALF - d, 1)
    keep = lane < HALF - d
    return jnp.where(keep, ra, rb), jnp.where(keep, rb, 0.0)


def z_minus(pair, d, lane):
    a, b = pair
    ra, rb = pltpu.roll(a, d, 1), pltpu.roll(b, d, 1)
    keep = lane >= d
    return jnp.where(keep, ra, 0.0), jnp.where(keep, rb, ra)


def second_z(pair, lane):
    out = [second_coef[0] * v for v in pair]
    for d in range(1, 5):
        up, down = z_plus(pair, d, lane), z_minus(pair, d, lane)
        out = [o + second_coef[d] * (u + w) for o, u, w in zip(out, up, down)]
    return out


def first_z(pair, lane):
    out = None
    for d in range(1, 5):
        up, down = z_plus(pair, d, lane), z_minus(pair, d, lane)
        term = [first_coef[d - 1] * (u - w) for u, w in zip(up, down)]
        out = term if out is None else [o + t for o, t in zip(out, term)]
    return out


def second_y(pair, row):
    out = []
    for f in pair:
        acc = second_coef[0] * f
        for d in range(1, 5):
            up = jnp.where(row < AY - d, pltpu.roll(f, AY - d, 0), 0.0)
            down = jnp.where(row >= d, pltpu.roll(f, d, 0), 0.0)
            acc = acc + second_coef[d] * (up + down)
        out.append(acc)
    return out


def x_parts(rows):
    second, first = [], []
    for s in range(2):
        acc = second_coef[0] * rows[4][s]
        der = None
        for d in range(1, 5):
            acc = acc + second_coef[d] * (rows[4 + d][s] + rows[4 - d][s])
            term = first_coef[d - 1] * (rows[4 + d][s] - rows[4 - d][s])
            der = term if der is None else der + term
        second.append(acc)
        first.append(der)
    return second, first


CORE, X_HI, BLOCK, FREE, STAYS, EVEN, KEEP, PARITY_LAST, PARITY_FREE = range(9)
PARITY, ROLE_TO, SIDE, SOURCE, OWNER, ROLE_FROM = 12, 16, 20, 24, 28, 32


def plan_values(ids, offsets):
    shot, aper = ids[0], ids[1]
    core, x_lo, x_hi = shot & 1, shot >> 1, aper & 1
    x = 2 * x_hi + x_lo
    z, y = aper >> 3, (aper >> 1) & 3
    even_z = 1 - (z & 1)
    block = 4 * z + jnp.where(even_z == 1, y, 3 - y)
    straight = 4 * z + y
    turns = [o & 31 for o in offsets]

    def of(values, g):
        return jnp.where(g < 2, jnp.where(g == 0, values[0], values[1]), jnp.where(g == 2, values[2], values[3]))

    def first(flags):
        return jnp.where(flags[0], 0, jnp.where(flags[1], 1, jnp.where(flags[2], 2, 3)))

    def group_of(x):
        return 2 * (x & 1) + (x >> 1)

    last = first([t == 31 for t in turns])
    free = 6 - first([o == 0 for o in offsets]) - first([o == 96 for o in offsets]) - last
    free_turn = of(turns, free)

    def role_of(g):
        return jnp.where(g == last, 1, jnp.where((g == free) & (free_turn != 0), 2, 0))

    def row_of(g):
        o = of(offsets, g)
        return (o + 2 * straight + (x_hi ^ (o & 1))) >> 5

    def parity_before(g):
        o = of(offsets, g)
        return ((o >> 5) + (2 * straight + x_hi < (o & 31)).astype(jnp.int32)) & 1

    group = group_of(x)
    offset = of(offsets, group)
    out = {
        CORE: core,
        X_HI: x_hi,
        BLOCK: block,
        FREE: free_turn,
        STAYS: (x_hi == core).astype(jnp.int32) * even_z,
        EVEN: even_z,
        KEEP: jnp.where(free_turn == 31, 1 - x_hi, jnp.where(free_turn == 1, x_hi, 0)),
        PARITY_LAST: parity_before(last),
        PARITY_FREE: parity_before(free),
    }
    for by in range(4):
        to, came = group_of((x + by) & 3), group_of((x - by) & 3)
        out[PARITY + by] = parity_before(to)
        out[ROLE_TO + by] = role_of(to)
        out[SIDE + by] = (((x + by) & 3) >> 1) ^ (offset & 1)
        out[OWNER + by] = row_of(came) - 2 * x_lo
        out[ROLE_FROM + by] = role_of(came)
    for h in range(2):
        row = (offset + 2 * block + h) >> 5
        out[SOURCE + h] = (x - (2 * (h ^ (offset & 1)) + (row >> 1))) & 3
    return out


def fetch(which, choices, sems):
    for k, (a, b, out) in enumerate(choices):

        @pl.when(which)
        def _(a=a, out=out, k=k):
            pltpu.make_async_copy(a, out, sems.at[k]).start()

        @pl.when(jnp.logical_not(which))
        def _(b=b, out=out, k=k):
            pltpu.make_async_copy(b, out, sems.at[k]).start()

    for k, (a, _, out) in enumerate(choices):
        pltpu.make_async_copy(a, out, sems.at[k]).wait()


def plan_kernel(ids, offsets, velocity, epsilon, delta, angle, plan, own, other, sems):
    values = plan_values(ids, [offsets[g] for g in range(4)])
    for k, v in values.items():
        plan[k] = v
    fetch(
        values[CORE] == 0,
        (
            (velocity, delta, own.at[0]),
            (epsilon, angle, own.at[1]),
            (delta, velocity, other.at[0]),
            (angle, epsilon, other.at[1]),
        ),
        sems,
    )


def state_kernel(plan, fwd_now, adj_now, fwd_before, adj_before, one, two, sems):
    fetch(
        plan[X_HI] == 0,
        (
            (adj_now.at[0], fwd_now.at[0], one.at[0]),
            (fwd_now.at[0], adj_now.at[0], two.at[0]),
            (adj_before.at[0], fwd_before.at[0], one.at[1]),
            (fwd_before.at[0], adj_before.at[0], two.at[1]),
        ),
        sems,
    )


def rows_kernel(plan, own, came, last, free):
    mine_last, mine_free = plan[PARITY_LAST] == plan[CORE], plan[PARITY_FREE] == plan[CORE]
    for f in range(2):
        for i in range(TX):
            a, b = own[f, i], came[f, i]
            last[f, i] = jnp.where(mine_last, a, b)
            free[f, i] = jnp.where(mine_free, a, b)


def send_kernel(plan, own, came, last, last_came, free, free_came, kept, one, two, *outs):
    first, stays = plan[CORE] == 0, plan[STAYS] == 1
    for t in range(2):
        lo, hi = outs[4 + 2 * t : 6 + 2 * t]
        for p in range(2):
            for i in range(TX):
                a, b = one[t, p, i], jnp.where(stays, kept[t, p, i], two[t, p, i])
                lo[p, i] = jnp.where(first, b, a)
                hi[p, i] = jnp.where(first, a, b)
    high = plan[X_HI] == 1
    keep = plan[KEEP] == 1
    mine = [plan[PARITY + by] == plan[CORE] for by in range(4)]
    role = [plan[ROLE_TO + by] for by in range(4)]
    for f in range(2):
        for i in range(TX):
            a, b = own[f, i], came[f, i]
            turned_last = jnp.where(high, last_came[f, i], last[f, i])
            turned_free = jnp.where(keep, free[f, i], free_came[f, i])
            for by in range(4):
                straight = jnp.where(mine[by], a, b)
                turned = jnp.where(role[by] == 1, turned_last, turned_free)
                outs[by][f, i] = jnp.where(role[by] == 0, straight, turned)


def tiles_kernel(plan, kept, got_0, got_1, got_2, got_3, out):
    even = plan[EVEN] == 1
    source = [plan[SOURCE + h] for h in range(2)]
    for f in range(2):
        for i in range(TX):
            rows = [jnp.where(even, kept[f, i], got_0[f, i]), got_1[f, i], got_2[f, i], got_3[f, i]]
            for h in range(2):
                a = jnp.where(source[h] == 0, rows[0], rows[1])
                b = jnp.where(source[h] == 2, rows[2], rows[3])
                out[h, f, i] = jnp.where(source[h] < 2, a, b)


def fill_rows(plan, lo, hi, low, high, ext):
    first, last = plan[BLOCK] == 0, plan[BLOCK] == 15
    for p in range(2):
        for i in range(TX):
            ext[p, i] = jnp.where(first, 0.0, low[p, i])
            ext[p, TX + i] = lo[p, i]
            ext[p, 2 * TX + i] = hi[p, i]
            ext[p, 3 * TX + i] = jnp.where(last, 0.0, high[p, i])


def step_kernel(plan, lo, hi, lo_b, hi_b, low, high, coef, inj, new_lo, new_hi, *rest):
    packed, ext = (rest[0], rest[1]) if len(rest) == 2 else (None, rest[0])
    fill_rows(plan, lo, hi, low, high, ext)
    for t, (back, mid, out) in enumerate(((lo_b, lo, new_lo), (hi_b, hi, new_hi))):

        def tile(i, carry, t=t, back=back, mid=mid, out=out):
            def emit(h, new_p, new_q):
                out[0, i, :, h] = new_p
                out[1, i, :, h] = new_q
                if packed is not None:
                    packed[0, t, i, :, h] = mid[0, i, :, h]
                    packed[1, t, i, :, h] = new_p

            one_row(ext, t * TX + i, lambda p, h: back[p, i, :, h], coef, inj, emit)
            return carry

        lax.fori_loop(0, TX, tile, 0)


def one_row(ext, i, before, coef, inj, emit):
    lane = lax.broadcasted_iota(jnp.int32, (AY, HALF), 1)
    row = lax.broadcasted_iota(jnp.int32, (AY, HALF), 0)
    halves = (pl.ds(0, HALF), pl.ds(HALF, HALF))
    parts = []
    for p in range(2):
        rows = [[ext[p, i + d, :, h] for h in halves] for d in range(9)]
        curve_x, slope_x = x_parts(rows)
        parts.append((rows[4], curve_x, second_z(rows[4], lane), first_z(slope_x, lane)))
    (mid_p, xp, zp, cp), (mid_q, xq, zq, cq) = parts
    yp = second_y(mid_p, row)
    for s, h in enumerate(halves):
        aniso, coupled, square = coef[0, i, :, h], coef[1, i, :, h], coef[2, i, :, h]
        sine, cosine, double = coef[3, i, :, h], coef[4, i, :, h], coef[5, i, :, h]
        axial_p = sine * xp[s] + cosine * zp[s] + double * cp[s]
        plane_p = xp[s] + yp[s] + zp[s] - axial_p
        axial_q = sine * xq[s] + cosine * zq[s] + double * cq[s]
        add = inj[i, :, h]
        new_p = 2.0 * mid_p[s] - before(0, h) + aniso * plane_p + coupled * axial_q + add
        new_q = 2.0 * mid_q[s] - before(1, h) + coupled * plane_p + square * axial_q + add
        emit(h, new_p, new_q)


def last_kernel(plan, lo, hi, lo_b, hi_b, low, high, coef, inj, other, keep, give, ext, part):
    fill_rows(plan, lo, hi, low, high, ext)
    for t, (back, mid) in enumerate(((lo_b, lo), (hi_b, hi))):

        def tile(i, carry, t=t, back=back, mid=mid):
            def emit(h, new_p, new_q):
                part[t, i, :, h] = new_p * other[0, t, i, :, h] + mid[0, i, :, h] * other[1, t, i, :, h]

            one_row(ext, t * TX + i, lambda p, h: back[p, i, :, h], coef, inj, emit)
            return carry

        lax.fori_loop(0, TX, tile, 0)
    first = plan[CORE] == 0
    for t in range(2):
        for i in range(TX):
            low_y, high_y = part[t, i, :HALF_Y], part[t, i, HALF_Y:]
            keep[t, i] = jnp.where(first, low_y, high_y)
            give[t, i] = jnp.where(first, high_y, low_y)


def total_kernel(plan, keep, came, *outs):
    for i in range(TX):
        lo = keep[0, i] + came[0, i]
        hi = keep[1, i] + came[1, i]
        for by in range(4):
            outs[by][i] = jnp.where(plan[SIDE + by] == 0, lo, hi)


def owners_kernel(plan, kept, got_0, got_1, got_2, got_3, straight, last, free):
    even = plan[EVEN] == 1
    for i in range(TX):
        parts = [jnp.where(even, kept[i], got_0[i]), got_1[i], got_2[i], got_3[i]]
        for k, out in enumerate((straight, last, free)):
            for core in range(2):
                acc = jnp.zeros_like(parts[0])
                for by in range(4):
                    ours = (plan[OWNER + by] == core) & (plan[ROLE_FROM + by] == k)
                    acc = acc + jnp.where(ours, parts[by], 0.0)
                out[core, i] = acc


def image_kernel(plan, straight, last, last_came, free_low, free_high, keep, give):
    high, first = plan[X_HI] == 1, plan[CORE] == 0
    for i in range(TX):
        sums = []
        for core in range(2):
            turned = jnp.where(high, last_came[core, i], last[core, i])
            free = jnp.where(high, free_high[core, i], free_low[core, i])
            sums.append(straight[core, i] + turned + free)
        keep[i] = jnp.where(first, sums[0], sums[1])
        give[i] = jnp.where(first, sums[1], sums[0])


def join_kernel(plan, keep, came, out):
    first = plan[CORE] == 0
    for i in range(TX):
        out[i, :HALF_Y] = jnp.where(first, keep[i], came[i])
        out[i, HALF_Y:] = jnp.where(first, came[i], keep[i])


def inject_kernel(plan, cells, amounts, out):
    x = cells[0:1, :] - 8 * plan[BLOCK]
    here = (x >= 0) & (x < 8)
    spot = jnp.where(here, x * AY + cells[1:2, :], -1)
    depth = cells[2:3, :]
    count = cells.shape[1]
    which = (lax.broadcasted_iota(jnp.int32, (8 * AY, count), 0) == spot).astype(F32)
    level = lax.broadcasted_iota(jnp.int32, (AZ, count), 0) == depth
    for k in range(STEPS):
        values = jnp.where(level, amounts[k : k + 1, :], 0.0)
        flat = lax.dot_general(
            which,
            values,
            (((1,), (1,)), ((), ())),
            precision=lax.Precision.HIGHEST,
            preferred_element_type=F32,
        )
        for i in range(8):
            out[k, i] = flat[i * AY : (i + 1) * AY, :]


def sine_cosine(angle):
    sq = angle * angle
    sine = -1.0 / 39916800.0
    for c in (1.0 / 362880.0, -1.0 / 5040.0, 1.0 / 120.0, -1.0 / 6.0, 1.0):
        sine = sine * sq + c
    cosine = 1.0 / 479001600.0
    for c in (-1.0 / 3628800.0, 1.0 / 40320.0, -1.0 / 720.0, 1.0 / 24.0, -0.5, 1.0):
        cosine = cosine * sq + c
    return sine * angle, cosine


def coef_kernel(plan, own, other, out):
    core = plan[CORE]
    for t in range(2):

        def tile(i, carry, t=t):
            mine = [own[t, f, i] for f in range(2)]
            theirs = [other[t, f, i] for f in range(2)]
            velocity = jnp.where(core == 0, mine[0], theirs[0])
            epsilon = jnp.where(core == 0, mine[1], theirs[1])
            delta = jnp.where(core == 0, theirs[0], mine[0])
            angle = jnp.where(core == 0, theirs[1], mine[1])
            square = velocity * velocity
            sine, cosine = sine_cosine(angle)
            k = t * TX + i
            out[0, k] = square * (1.0 + 2.0 * epsilon)
            out[1, k] = square * jnp.sqrt(1.0 + 2.0 * delta)
            out[2, k] = square
            out[3, k] = sine * sine
            out[4, k] = cosine * cosine
            out[5, k] = 2.0 * sine * cosine
            return carry

        lax.fori_loop(0, TX, tile, 0)


ANY = pl.BlockSpec(memory_space=pl.ANY)
LIMIT = pltpu.CompilerParams(vmem_limit_bytes=32 * 1024 * 1024)


def call(kernel, n_in, outs, scratch=()):
    return pl.pallas_call(
        kernel,
        out_shape=[jax.ShapeDtypeStruct(s, F32) for s in outs],
        in_specs=[SMEM] + [VMEM] * n_in,
        out_specs=[VMEM] * len(outs),
        scratch_shapes=[pltpu.VMEM(s, F32) for s in scratch],
        compiler_params=LIMIT,
    )


TILE = (2, TX, AY, AZ)
PART = (TX, HALF_Y, AZ)


def roll(value, by, avoid):
    by = by % 16
    if by == 0:
        return value
    if by == avoid:
        return roll(roll(value, 8, avoid), by - 8, avoid)
    return send(value, rolled(by, by))


def turn_model(value, x_hi, r):
    low, high = -((r + 1) // 2), -(r // 2)
    if r in (0, 1, 31) or r % 2 == 0:
        return roll(value, high if r != 1 else low, 1)
    if r in (3, 5, 27, 29):
        return jnp.where(x_hi == 1, roll(value, high, 1), roll(value, low, 1))
    return send(value, rolled(low, high))


def turn_image(value, r):
    low = roll(value, (r + 1) // 2, 15)
    return low, low if r % 2 == 0 else roll(value, r // 2, 15)


def local(
    velocity,
    thomsen_epsilon,
    thomsen_delta,
    tilt_angle,
    fwd_now,
    fwd_before,
    adj_now,
    adj_before,
    wavelet,
    traces,
    offsets,
    source_cell,
    receiver_cell,
):
    shot, aper = lax.axis_index("shot"), lax.axis_index("aper")
    ids = jnp.stack([shot, aper]).astype(jnp.int32)
    swap, up, down = other_core(), along_path(1), along_path(-1)

    plan, own, other = pl.pallas_call(
        plan_kernel,
        out_shape=[jax.ShapeDtypeStruct((40,), jnp.int32)] + [jax.ShapeDtypeStruct(TILE, F32)] * 2,
        in_specs=[SMEM] * 2 + [ANY] * 4,
        out_specs=[SMEM, VMEM, VMEM],
        scratch_shapes=[pltpu.SemaphoreType.DMA((4,))],
        compiler_params=LIMIT,
    )(ids, offsets, velocity, thomsen_epsilon, thomsen_delta, tilt_angle)
    came = send(other, swap)
    one, two = pl.pallas_call(
        state_kernel,
        out_shape=[jax.ShapeDtypeStruct((2,) + TILE, F32)] * 2,
        in_specs=[SMEM] + [ANY] * 4,
        out_specs=[VMEM] * 2,
        scratch_shapes=[pltpu.SemaphoreType.DMA((4,))],
        compiler_params=LIMIT,
    )(plan, fwd_now, adj_now, fwd_before, adj_before)
    got_one, got_two = send(one, state_first()), send(two, state_second())

    last, free = call(rows_kernel, 2, [TILE] * 2)(plan, own, came)
    last_came = send(last, rolled(1, 1))
    free_came = lax.switch(
        plan[FREE], [lambda v, r=r: turn_model(v, aper % 2, r) for r in range(32)], free
    )
    *rows, lo, hi, lo_b, hi_b = call(send_kernel, 9, [TILE] * 8)(
        plan, own, came, last, last_came, free, free_came, two, got_one, got_two
    )
    got = [send(rows[by], across(by)) for by in range(4)]
    tiles = call(tiles_kernel, 5, [(2,) + TILE])(plan, rows[0], *got)[0]
    coef = call(coef_kernel, 2, [(6, 8, AY, AZ)])(plan, tiles, send(tiles, swap))[0]

    n_rec = receiver_cell.shape[1]
    group = 2 * (shot // 2) + aper % 2
    rec = receiver_cell[group].T
    at_first = jnp.arange(n_rec)[None, :] == 0
    src = jnp.where(at_first, source_cell[group][:, None], -1000)
    pulse = jnp.where(at_first, wavelet[group][:, None], 0.0)
    forward = shot % 2 == 0
    cells = jnp.where(forward, src, rec)
    amounts = jnp.where(forward, pulse, traces[group])
    inj = call(inject_kernel, 2, [(STEPS, 8, AY, AZ)])(plan, cells, amounts)[0]

    shared = None
    for k in range(STEPS - 1):
        low, high = send(hi, up), send(lo, down)
        outs = [TILE, TILE] + ([(2, 2, TX, AY, AZ)] if k == 1 else [])
        new = call(step_kernel, 8, outs, [(2, 4 * TX, AY, AZ)])(
            plan, lo, hi, lo_b, hi_b, low, high, coef, inj[k]
        )
        if k == 1:
            shared = send(new[2], swap)
        lo_b, hi_b, lo, hi = lo, hi, new[0], new[1]
    low, high = send(hi, up), send(lo, down)
    keep, give = call(
        last_kernel, 9, [(2,) + PART] * 2, [(2, 4 * TX, AY, AZ), (2, TX, AY, AZ)]
    )(plan, lo, hi, lo_b, hi_b, low, high, coef, inj[STEPS - 1], shared)

    parts = call(total_kernel, 2, [PART] * 4)(plan, keep, send(give, swap))
    got = [send(parts[by], across(by)) for by in range(4)]
    straight, last, free = call(owners_kernel, 5, [(2,) + PART] * 3)(plan, parts[0], *got)
    last_came = send(last, rolled(15, 15))
    free_low, free_high = lax.switch(plan[FREE], [lambda v, r=r: turn_image(v, r) for r in range(32)], free)
    keep, give = call(image_kernel, 5, [PART] * 2)(plan, straight, last, last_came, free_low, free_high)
    return call(join_kernel, 2, [(TX, AY, AZ)])(plan, keep, send(give, swap))[0]


def solution(mesh):
    model = P(("shot", "aper"), None, None)
    field = P("shot", None, "aper", None, None)
    return jax.shard_map(
        local,
        mesh=mesh,
        in_specs=(model,) * 4 + (field,) * 4 + (P(),) * 5,
        out_specs=model,
        check_vma=False,
    )
```

profile of v0, /device:TPU:1, one launch (start us, length us, event | category | flops | bytes accessed | tf_op | source)
XLA Modules:
  0.0 185.4 jit_solution(13079703177841244700)
XLA Ops:
  0.1 0.9 copy-done.9
  1.0 0.9 copy-done.10
  1.9 0.9 copy-done.11
  2.8 0.9 copy-done.12
  4.4 2.1 %shard_map.127 = (s32[40]{0:T(128)S(1)}, f32[2,4,32,256]{3,2,1,0:T(8,128)S(1)}, f32[2,4,32,256]{3,2,1,0:T(8,128)S(1)}) custom-call(s32[2]{0:T(128)S(1)} %pad_add_fusion.ids, s32[4]{0:T(128)S(1)} %copy-done.13, f32[4,32,256]{2,1,0:T(8,128)S(1)} %copy-done.9, f32[4,32,256]{2,1,0:T(8,128)S(1)} %copy-done.10, f32[4,32,256]{2,1,0:T(8,128)S(1)} %copy-done.11, ...), custom_call_target="tpu_custom_call" | custom-call | tf_op jit(solution)/shard_map/pallas_call | solution.py:542
  6.5 1.5 collective-permute-start.86
  8.0 0.9 copy-done.1
  8.9 0.9 copy-done.2
  9.9 0.9 copy-done.3
  10.8 0.9 copy-done.4
  12.4 2.8 %collective-permute-start.89 = (f32[2,2,4,32,256]{4,3,2,1,0:T(8,128)S(1)}, f32[2,2,4,32,256]{4,3,2,1,0:T(8,128)S(1)}, u32[]{:S(2)}, u32[]{:S(2)}) collective-permute-start(f32[2,2,4,32,256]{4,3,2,1,0:T(8,128)S(1)} %get-tuple-element.162.kept), channel_id=1, source_target_pairs={{0,6},{8,14},{16,22},{24,30},{2,4},{10,12},{18,20},{26,28},{4,2},{... | collective-permute-start | bytes 1572872 | tf_op jit(solution)/shard_map/ppermute | solution.py:52
  15.3 2.8 %collective-permute-start.88 = (f32[2,2,4,32,256]{4,3,2,1,0:T(8,128)S(1)}, f32[2,2,4,32,256]{4,3,2,1,0:T(8,128)S(1)}, u32[]{:S(2)}, u32[]{:S(2)}) collective-permute-start(f32[2,2,4,32,256]{4,3,2,1,0:T(8,128)S(1)} %get-tuple-element.163), channel_id=1, source_target_pairs={{0,32},{8,46},{16,48},{24,62},{2,34},{10,44},{18,50},{26,60},{4,36... | collective-permute-start | bytes 1572872 | tf_op jit(solution)/shard_map/ppermute | solution.py:52
  18.1 1.3 shard_map.128
  20.7 31.5 %conditional.2 = (f32[2,4,32,256]{3,2,1,0:T(8,128)}) conditional(s32[]{:T(128)} %bitcast.2, f32[2,4,32,256]{3,2,1,0:T(8,128)} %get-tuple-element.161.free, f32[2,4,32,256]{3,2,1,0:T(8,128)} %get-tuple-element.161.free, f32[2,4,32,256]{3,2,1,0:T(8,128)} %get-tuple-element.161.free, (s32[]{:T(128)}, ...), branch_computations={%region_0.0_spmd, %region_1.0_spmd, %region_2.0_spmd, %region_3.4_... | conditional | flops 65548 | bytes 3932407 | solution.py:563
  20.7 3.9 %collective-permute-start.81 = (f32[2,4,32,256]{3,2,1,0:T(8,128)}, f32[2,4,32,256]{3,2,1,0:T(8,128)S(1)}, u32[]{:S(2)}, u32[]{:S(2)}) collective-permute-start(f32[2,4,32,256]{3,2,1,0:T(8,128)} %get-tuple-element.119), channel_id=1, source_target_pairs={{0,6},{8,14},{16,22},{24,30},{2,8},{10,16},{18,24},{26,0},{4,10},{... | collective-permute-start | bytes 786440 | tf_op jit(solution)/shard_map/cond/branch_27_fun/ppermute | solution.py:52
  25.0 6.7 %collective-permute-done.81 = f32[2,4,32,256]{3,2,1,0:T(8,128)S(1)} collective-permute-done((f32[2,4,32,256]{3,2,1,0:T(8,128)}, f32[2,4,32,256]{3,2,1,0:T(8,128)S(1)}, u32[]{:S(2)}, u32[]{:S(2)}) %collective-permute-start.81) | collective-permute-done | bytes 262176 | tf_op jit(solution)/shard_map/cond/branch_27_fun/ppermute | solution.py:52
  31.7 7.6 %collective-permute-done.82 = f32[2,4,32,256]{3,2,1,0:T(8,128)} collective-permute-done((f32[2,4,32,256]{3,2,1,0:T(8,128)}, f32[2,4,32,256]{3,2,1,0:T(8,128)}, u32[]{:S(2)}, u32[]{:S(2)}) %collective-permute-start.82) | collective-permute-done | bytes 262176 | tf_op jit(solution)/shard_map/cond/branch_27_fun/ppermute | solution.py:52
  39.3 1.7 broadcast_select_fusion.2
  52.2 0.7 copy-done.7
  52.9 0.9 copy-done.6
  53.9 0.9 copy-done.8
  54.8 2.1 %shard_map.130 = (f32[2,4,32,256]{3,2,1,0:T(8,128)S(1)}, f32[2,4,32,256]{3,2,1,0:T(8,128)}, f32[2,4,32,256]{3,2,1,0:T(8,128)}, f32[2,4,32,256]{3,2,1,0:T(8,128)}...) custom-call(s32[40]{0:T(128)S(1)} %get-tuple-element.157.plan, ...), custom_call_target="tpu_custom_call" | custom-call | tf_op jit(solution)/shard_map/pallas_call | solution.py:566
  56.9 4.4 %collective-permute-start.92 = (f32[2,4,32,256]{3,2,1,0:T(8,128)S(1)}, f32[2,4,32,256]{3,2,1,0:T(8,128)S(1)}, u32[]{:S(2)}, u32[]{:S(2)}) collective-permute-start(f32[2,4,32,256]{3,2,1,0:T(8,128)S(1)} %get-tuple-element.168.kept), channel_id=1, source_target_pairs={{0,6},{8,14},{16,22},{24,30},{2,4},{10,12},{18,20},{26,28},{4,2},{... | collective-permute-start | bytes 786440 | tf_op jit(solution)/shard_map/ppermute | solution.py:52
  61.7 0.9 collective-permute-start.94
  62.6 1.5 collective-permute-start.95
  64.1 0.7 fusion
  64.8 1.8 collective-permute-done.92.got_0
  66.6 4.0 %collective-permute-done.93.got_1 = f32[2,4,32,256]{3,2,1,0:T(8,128)S(1)} collective-permute-done((f32[2,4,32,256]{3,2,1,0:T(8,128)}, f32[2,4,32,256]{3,2,1,0:T(8,128)S(1)}, u32[]{:S(2)}, u32[]{:S(2)}) %collective-permute-start.93) | collective-permute-done | bytes 262176 | tf_op jit(solution)/shard_map/ppermute | solution.py:52
  70.6 2.5 %collective-permute-done.94.got_2 = f32[2,4,32,256]{3,2,1,0:T(8,128)S(1)} collective-permute-done((f32[2,4,32,256]{3,2,1,0:T(8,128)}, f32[2,4,32,256]{3,2,1,0:T(8,128)S(1)}, u32[]{:S(2)}, u32[]{:S(2)}) %collective-permute-start.94) | collective-permute-done | bytes 262176 | tf_op jit(solution)/shard_map/ppermute | solution.py:52
  73.1 2.6 %collective-permute-done.95.got_3 = f32[2,4,32,256]{3,2,1,0:T(8,128)S(1)} collective-permute-done((f32[2,4,32,256]{3,2,1,0:T(8,128)}, f32[2,4,32,256]{3,2,1,0:T(8,128)S(1)}, u32[]{:S(2)}, u32[]{:S(2)}) %collective-permute-start.95) | collective-permute-done | bytes 262176 | tf_op jit(solution)/shard_map/ppermute | solution.py:52
  76.3 2.1 %collective-permute-start.96 = (f32[2,2,4,32,256]{4,3,2,1,0:T(8,128)S(1)}, f32[2,2,4,32,256]{4,3,2,1,0:T(8,128)S(1)}, u32[]{:S(2)}, u32[]{:S(2)}) collective-permute-start(f32[2,2,4,32,256]{4,3,2,1,0:T(8,128)S(1)} %shard_map.131.own), channel_id=1, source_target_pairs={{0,32},{8,40},{16,48},{24,56},{2,34},{10,42},{18,50},{26,58},{4,36... | collective-permute-start | bytes 1572872 | tf_op jit(solution)/shard_map/ppermute | solution.py:52
  78.5 0.7 fusion.1
  79.1 8.7 %collective-permute-start.90 = (f32[2,4,32,256]{3,2,1,0:T(8,128)S(1)}, f32[2,4,32,256]{3,2,1,0:T(8,128)S(1)}, u32[]{:S(2)}, u32[]{:S(2)}) collective-permute-start(f32[2,4,32,256]{3,2,1,0:T(8,128)S(1)} %get-tuple-element.165.hi.hi_b), channel_id=1, source_target_pairs={{0,2},{8,16},{16,18},{24,0},{2,4},{10,8},{18,20},{26,24},{4,6},{12... | collective-permute-start | bytes 786440 | tf_op jit(solution)/shard_map/ppermute | solution.py:52
  87.8 10.3 %collective-permute-start.91 = (f32[2,4,32,256]{3,2,1,0:T(8,128)S(1)}, f32[2,4,32,256]{3,2,1,0:T(8,128)S(1)}, u32[]{:S(2)}, u32[]{:S(2)}) collective-permute-start(f32[2,4,32,256]{3,2,1,0:T(8,128)S(1)} %get-tuple-element.164.lo.lo_b), channel_id=1, source_target_pairs={{0,24},{8,10},{16,8},{24,26},{2,0},{10,12},{18,16},{26,28},{4,2},{... | collective-permute-start | bytes 786440 | tf_op jit(solution)/shard_map/ppermute | solution.py:52
  98.1 0.8 bitcast_select_fusion.1.amounts
  98.9 1.6 shard_map.133
  100.7 1.0 shard_map.132.coef
  101.7 3.1 %collective-permute-done.90.low = f32[2,4,32,256]{3,2,1,0:T(8,128)S(1)} collective-permute-done((f32[2,4,32,256]{3,2,1,0:T(8,128)S(1)}, f32[2,4,32,256]{3,2,1,0:T(8,128)S(1)}, u32[]{:S(2)}, u32[]{:S(2)}) %collective-permute-start.90) | collective-permute-done | bytes 262176 | tf_op jit(solution)/shard_map/ppermute | solution.py:52
  104.8 3.6 %shard_map.134 = (f32[2,4,32,256]{3,2,1,0:T(8,128)S(1)}, f32[2,4,32,256]{3,2,1,0:T(8,128)S(1)}) custom-call(s32[40]{0:T(128)S(1)} %get-tuple-element.157.plan, f32[2,4,32,256]{3,2,1,0:T(8,128)S(1)} %get-tuple-element.164.lo.lo_b, f32[2,4,32,256]{3,2,1,0:T(8,128)S(1)} %get-tuple-element.165.hi.hi_b, f32[2,4,32,256]{3,2,1,0:T(8,128)S(1)} %get-tuple-element.166.lo_b, ...), custom_call_target="tpu_custom_call" | custom-call | tf_op jit(solution)/shard_map/pallas_call | solution.py:588
  108.5 2.7 %collective-permute-start.98 = (f32[2,4,32,256]{3,2,1,0:T(8,128)S(1)}, f32[2,4,32,256]{3,2,1,0:T(8,128)S(1)}, u32[]{:S(2)}, u32[]{:S(2)}) collective-permute-start(f32[2,4,32,256]{3,2,1,0:T(8,128)S(1)} %get-tuple-element.172.lo.lo_b), channel_id=1, source_target_pairs={{0,24},{8,10},{16,8},{24,26},{2,0},{10,12},{18,16},{26,28},{4,2},{... | collective-permute-start | bytes 786440 | tf_op jit(solution)/shard_map/ppermute | solution.py:52
  111.2 5.8 %collective-permute-done.97.low = f32[2,4,32,256]{3,2,1,0:T(8,128)S(1)} collective-permute-done((f32[2,4,32,256]{3,2,1,0:T(8,128)S(1)}, f32[2,4,32,256]{3,2,1,0:T(8,128)S(1)}, u32[]{:S(2)}, u32[]{:S(2)}) %collective-permute-start.97) | collective-permute-done | bytes 262176 | tf_op jit(solution)/shard_map/ppermute | solution.py:52
  116.9 3.6 %shard_map.135 = (f32[2,4,32,256]{3,2,1,0:T(8,128)S(1)}, f32[2,4,32,256]{3,2,1,0:T(8,128)S(1)}, f32[2,2,4,32,256]{4,3,2,1,0:T(8,128)S(1)}) custom-call(s32[40]{0:T(128)S(1)} %get-tuple-element.157.plan, f32[2,4,32,256]{3,2,1,0:T(8,128)S(1)} %get-tuple-element.172.lo.lo_b, f32[2,4,32,256]{3,2,1,0:T(8,128)S(1)} %get-tuple-element.173.hi.hi_b, ...), custom_call_target="tpu_custom_call" | custom-call | tf_op jit(solution)/shard_map/pallas_call | solution.py:588
  120.6 2.4 %collective-permute-start.100 = (f32[2,4,32,256]{3,2,1,0:T(8,128)S(1)}, f32[2,4,32,256]{3,2,1,0:T(8,128)S(1)}, u32[]{:S(2)}, u32[]{:S(2)}) collective-permute-start(f32[2,4,32,256]{3,2,1,0:T(8,128)S(1)} %get-tuple-element.174.lo.lo_b), channel_id=1, source_target_pairs={{0,24},{8,10},{16,8},{24,26},{2,0},{10,12},{18,16},{26,28},{4,2},{... | collective-permute-start | bytes 786440 | tf_op jit(solution)/shard_map/ppermute | solution.py:52
  123.0 2.1 %collective-permute-start.103 = (f32[2,2,4,32,256]{4,3,2,1,0:T(8,128)S(1)}, f32[2,2,4,32,256]{4,3,2,1,0:T(8,128)S(1)}, u32[]{:S(2)}, u32[]{:S(2)}) collective-permute-start(f32[2,2,4,32,256]{4,3,2,1,0:T(8,128)S(1)} %get-tuple-element.178), channel_id=1, source_target_pairs={{0,32},{8,40},{16,48},{24,56},{2,34},{10,42},{18,50},{26,58},{4,36... | collective-permute-start | bytes 1572872 | tf_op jit(solution)/shard_map/ppermute | solution.py:52
  125.0 1.9 %collective-permute-done.100.high = f32[2,4,32,256]{3,2,1,0:T(8,128)S(1)} collective-permute-done((f32[2,4,32,256]{3,2,1,0:T(8,128)S(1)}, f32[2,4,32,256]{3,2,1,0:T(8,128)S(1)}, u32[]{:S(2)}, u32[]{:S(2)}) %collective-permute-start.100) | collective-permute-done | bytes 262176 | tf_op jit(solution)/shard_map/ppermute | solution.py:52
  127.0 3.0 %collective-permute-done.99.low = f32[2,4,32,256]{3,2,1,0:T(8,128)S(1)} collective-permute-done((f32[2,4,32,256]{3,2,1,0:T(8,128)S(1)}, f32[2,4,32,256]{3,2,1,0:T(8,128)S(1)}, u32[]{:S(2)}, u32[]{:S(2)}) %collective-permute-start.99) | collective-permute-done | bytes 262176 | tf_op jit(solution)/shard_map/ppermute | solution.py:52
  129.9 3.6 %shard_map.136 = (f32[2,4,32,256]{3,2,1,0:T(8,128)S(1)}, f32[2,4,32,256]{3,2,1,0:T(8,128)S(1)}) custom-call(s32[40]{0:T(128)S(1)} %get-tuple-element.157.plan, f32[2,4,32,256]{3,2,1,0:T(8,128)S(1)} %get-tuple-element.174.lo.lo_b, f32[2,4,32,256]{3,2,1,0:T(8,128)S(1)} %get-tuple-element.175.hi.hi_b, f32[2,4,32,256]{3,2,1,0:T(8,128)S(1)} %get-tuple-element.172.lo.lo_b, ...), custom_call_target="tpu_custom_call" | custom-call | tf_op jit(solution)/shard_map/pallas_call | solution.py:588
  133.6 2.7 %collective-permute-start.102 = (f32[2,4,32,256]{3,2,1,0:T(8,128)S(1)}, f32[2,4,32,256]{3,2,1,0:T(8,128)S(1)}, u32[]{:S(2)}, u32[]{:S(2)}) collective-permute-start(f32[2,4,32,256]{3,2,1,0:T(8,128)S(1)} %get-tuple-element.176.lo), channel_id=1, source_target_pairs={{0,24},{8,10},{16,8},{24,26},{2,0},{10,12},{18,16},{26,28},{4,2},{... | collective-permute-start | bytes 786440 | tf_op jit(solution)/shard_map/ppermute | solution.py:52
  136.3 3.8 %collective-permute-done.101.low = f32[2,4,32,256]{3,2,1,0:T(8,128)S(1)} collective-permute-done((f32[2,4,32,256]{3,2,1,0:T(8,128)S(1)}, f32[2,4,32,256]{3,2,1,0:T(8,128)S(1)}, u32[]{:S(2)}, u32[]{:S(2)}) %collective-permute-start.101) | collective-permute-done | bytes 262176 | tf_op jit(solution)/shard_map/ppermute | solution.py:52
  140.0 3.6 %shard_map.137 = (f32[2,4,16,256]{3,2,1,0:T(8,128)S(1)}, f32[2,4,16,256]{3,2,1,0:T(8,128)S(1)}) custom-call(s32[40]{0:T(128)S(1)} %get-tuple-element.157.plan, f32[2,4,32,256]{3,2,1,0:T(8,128)S(1)} %get-tuple-element.176.lo, f32[2,4,32,256]{3,2,1,0:T(8,128)S(1)} %get-tuple-element.177.hi, f32[2,4,32,256]{3,2,1,0:T(8,128)S(1)} %get-tuple-element.174.lo.lo_b, ...), custom_call_target="tpu_custom_call" | custom-call | tf_op jit(solution)/shard_map/pallas_call | solution.py:595
  143.6 4.2 %collective-permute-start.104 = (f32[2,4,16,256]{3,2,1,0:T(8,128)S(1)}, f32[2,4,16,256]{3,2,1,0:T(8,128)S(1)}, u32[]{:S(2)}, u32[]{:S(2)}) collective-permute-start(f32[2,4,16,256]{3,2,1,0:T(8,128)S(1)} %get-tuple-element.180), channel_id=1, source_target_pairs={{0,32},{8,40},{16,48},{24,56},{2,34},{10,42},{18,50},{26,58},{4,36... | collective-permute-start | bytes 393224 | tf_op jit(solution)/shard_map/ppermute | solution.py:52
  147.8 1.0 collective-permute-done.104.came
  149.6 1.2 collective-permute-start.107
  150.7 2.0 %collective-permute-start.108 = (f32[4,16,256]{2,1,0:T(8,128)S(1)}, f32[4,16,256]{2,1,0:T(8,128)S(1)}, u32[]{:S(2)}, u32[]{:S(2)}) collective-permute-start(f32[4,16,256]{2,1,0:T(8,128)S(1)} %get-tuple-element.184), channel_id=1, source_target_pairs={{0,65},{8,79},{16,81},{24,95},{2,67},{10,77},{18,83},{26,93},{4,69... | collective-permute-start | bytes 196616 | tf_op jit(solution)/shard_map/ppermute | solution.py:52
  152.7 1.1 collective-permute-done.105.got_0
  153.8 2.0 %collective-permute-done.106.got_1 = f32[4,16,256]{2,1,0:T(8,128)S(1)} collective-permute-done((f32[4,16,256]{2,1,0:T(8,128)S(1)}, f32[4,16,256]{2,1,0:T(8,128)S(1)}, u32[]{:S(2)}, u32[]{:S(2)}) %collective-permute-start.106) | collective-permute-done | bytes 65568 | tf_op jit(solution)/shard_map/ppermute | solution.py:52
  156.5 7.9 %collective-permute-start.109 = (f32[2,4,16,256]{3,2,1,0:T(8,128)S(1)}, f32[2,4,16,256]{3,2,1,0:T(8,128)S(1)}, u32[]{:S(2)}, u32[]{:S(2)}) collective-permute-start(f32[2,4,16,256]{3,2,1,0:T(8,128)S(1)} %get-tuple-element.186.last), channel_id=1, source_target_pairs={{0,30},{8,6},{16,14},{24,22},{2,0},{10,8},{18,16},{26,24},{4,2},{1... | collective-permute-start | bytes 393224 | tf_op jit(solution)/shard_map/ppermute | solution.py:52
  164.4 14.7 %conditional.3 = (f32[2,4,16,256]{3,2,1,0:T(8,128)}, f32[2,4,16,256]{3,2,1,0:T(8,128)}) conditional(s32[]{:T(128)} %bitcast.2, f32[2,4,16,256]{3,2,1,0:T(8,128)S(1)} %get-tuple-element.187, f32[2,4,16,256]{3,2,1,0:T(8,128)S(1)} %get-tuple-element.187, f32[2,4,16,256]{3,2,1,0:T(8,128)S(1)} %get-tuple-element.187, ...), branch_computations={%region_32.33_spmd, %region_33.34_spmd, %region_34.35_spmd, %regio... | conditional | bytes 1573000 | solution.py:603
  171.9 5.4 %collective-permute-done.67 = f32[2,4,16,256]{3,2,1,0:T(8,128)} collective-permute-done((f32[2,4,16,256]{3,2,1,0:T(8,128)S(1)}, f32[2,4,16,256]{3,2,1,0:T(8,128)}, u32[]{:S(2)}, u32[]{:S(2)}) %collective-permute-start.67) | collective-permute-done | bytes 131104 | tf_op jit(solution)/shard_map/cond/branch_27_fun/ppermute | solution.py:52
  177.3 1.8 collective-permute-done.68
  179.1 1.0 shard_map.140
  180.1 2.9 %collective-permute-start.110 = (f32[4,16,256]{2,1,0:T(8,128)S(1)}, f32[4,16,256]{2,1,0:T(8,128)S(1)}, u32[]{:S(2)}, u32[]{:S(2)}) collective-permute-start(f32[4,16,256]{2,1,0:T(8,128)S(1)} %get-tuple-element.191), channel_id=1, source_target_pairs={{0,32},{8,40},{16,48},{24,56},{2,34},{10,42},{18,50},{26,58},{4,36... | collective-permute-start | bytes 196616 | tf_op jit(solution)/shard_map/ppermute | solution.py:52
  183.0 0.9 collective-permute-done.110.came
  183.9 1.2 shard_map.141
  (49 shorter events, 5.3 us)
Async XLA Ops:
  0.0 20.6 %copy-start = (s32[4,256,3]{1,0,2:T(4,128)S(1)}, s32[4,256,3]{1,0,2:T(4,128)}, u32[]{:S(2)}) copy-start(s32[4,256,3]{1,0,2:T(4,128)} %param.89) | copy-start | bytes 36868
  0.1 0.9 copy-start.9
  1.0 0.9 copy-start.10
  1.9 0.9 copy-start.11
  2.8 0.9 copy-start.12
  3.7 0.7 copy-start.13
  6.5 11.6 %collective-permute-start.86 = (f32[2,4,32,256]{3,2,1,0:T(8,128)S(1)}, f32[2,4,32,256]{3,2,1,0:T(8,128)S(1)}, u32[]{:S(2)}, u32[]{:S(2)}) collective-permute-start(f32[2,4,32,256]{3,2,1,0:T(8,128)S(1)} %get-tuple-element.159), channel_id=1, source_target_pairs={{0,32},{8,40},{16,48},{24,56},{2,34},{10,42},{18,50},{26,58},{4,36... | collective-permute-start | bytes 786440 | tf_op jit(solution)/shard_map/ppermute | solution.py:52
  8.0 0.9 copy-start.1
  8.9 0.9 copy-start.2
  9.9 0.9 copy-start.3
  10.8 0.9 copy-start.4
  12.4 40.5 %collective-permute-start.89 = (f32[2,2,4,32,256]{4,3,2,1,0:T(8,128)S(1)}, f32[2,2,4,32,256]{4,3,2,1,0:T(8,128)S(1)}, u32[]{:S(2)}, u32[]{:S(2)}) collective-permute-start(f32[2,2,4,32,256]{4,3,2,1,0:T(8,128)S(1)} %get-tuple-element.162.kept), channel_id=1, source_target_pairs={{0,6},{8,14},{16,22},{24,30},{2,4},{10,12},{18,20},{26,28},{4,2},{... | collective-permute-start | bytes 1572872 | tf_op jit(solution)/shard_map/ppermute | solution.py:52
  15.3 37.7 %collective-permute-start.88 = (f32[2,2,4,32,256]{4,3,2,1,0:T(8,128)S(1)}, f32[2,2,4,32,256]{4,3,2,1,0:T(8,128)S(1)}, u32[]{:S(2)}, u32[]{:S(2)}) collective-permute-start(f32[2,2,4,32,256]{4,3,2,1,0:T(8,128)S(1)} %get-tuple-element.163), channel_id=1, source_target_pairs={{0,32},{8,46},{16,48},{24,62},{2,34},{10,44},{18,50},{26,60},{4,36... | collective-permute-start | bytes 1572872 | tf_op jit(solution)/shard_map/ppermute | solution.py:52
  19.4 1.3 copy-start.5
  19.4 32.8 %collective-permute-start.87 = (f32[2,4,32,256]{3,2,1,0:T(8,128)S(1)}, f32[2,4,32,256]{3,2,1,0:T(8,128)S(1)}, u32[]{:S(2)}, u32[]{:S(2)}) collective-permute-start(f32[2,4,32,256]{3,2,1,0:T(8,128)S(1)} %get-tuple-element.160.last), channel_id=1, source_target_pairs={{0,2},{8,10},{16,18},{24,26},{2,4},{10,12},{18,20},{26,28},{4,6},{... | collective-permute-start | bytes 786440 | tf_op jit(solution)/shard_map/ppermute | solution.py:52
  20.7 10.9 %collective-permute-start.81 = (f32[2,4,32,256]{3,2,1,0:T(8,128)}, f32[2,4,32,256]{3,2,1,0:T(8,128)S(1)}, u32[]{:S(2)}, u32[]{:S(2)}) collective-permute-start(f32[2,4,32,256]{3,2,1,0:T(8,128)} %get-tuple-element.119), channel_id=1, source_target_pairs={{0,6},{8,14},{16,22},{24,30},{2,8},{10,16},{18,24},{26,0},{4,10},{... | collective-permute-start | bytes 786440 | tf_op jit(solution)/shard_map/cond/branch_27_fun/ppermute | solution.py:52
  24.6 14.6 %collective-permute-start.82 = (f32[2,4,32,256]{3,2,1,0:T(8,128)}, f32[2,4,32,256]{3,2,1,0:T(8,128)}, u32[]{:S(2)}, u32[]{:S(2)}) collective-permute-start(f32[2,4,32,256]{3,2,1,0:T(8,128)} %get-tuple-element.119), channel_id=1, source_target_pairs={{0,4},{8,12},{16,20},{24,28},{2,6},{10,14},{18,22},{26,30},{4,8},{... | collective-permute-start | bytes 786440 | tf_op jit(solution)/shard_map/cond/branch_27_fun/ppermute | solution.py:52
  52.2 0.7 copy-start.7
  52.9 1.0 copy-start.6
  53.9 0.9 copy-start.8
  56.9 9.7 %collective-permute-start.92 = (f32[2,4,32,256]{3,2,1,0:T(8,128)S(1)}, f32[2,4,32,256]{3,2,1,0:T(8,128)S(1)}, u32[]{:S(2)}, u32[]{:S(2)}) collective-permute-start(f32[2,4,32,256]{3,2,1,0:T(8,128)S(1)} %get-tuple-element.168.kept), channel_id=1, source_target_pairs={{0,6},{8,14},{16,22},{24,30},{2,4},{10,12},{18,20},{26,28},{4,2},{... | collective-permute-start | bytes 786440 | tf_op jit(solution)/shard_map/ppermute | solution.py:52
  61.4 9.2 %collective-permute-start.93 = (f32[2,4,32,256]{3,2,1,0:T(8,128)}, f32[2,4,32,256]{3,2,1,0:T(8,128)S(1)}, u32[]{:S(2)}, u32[]{:S(2)}) collective-permute-start(f32[2,4,32,256]{3,2,1,0:T(8,128)} %get-tuple-element.169), channel_id=1, source_target_pairs={{0,64},{8,78},{16,80},{24,94},{2,66},{10,76},{18,82},{26,92},{4,68... | collective-permute-start | bytes 786440 | tf_op jit(solution)/shard_map/ppermute | solution.py:52
  61.7 11.4 %collective-permute-start.94 = (f32[2,4,32,256]{3,2,1,0:T(8,128)}, f32[2,4,32,256]{3,2,1,0:T(8,128)S(1)}, u32[]{:S(2)}, u32[]{:S(2)}) collective-permute-start(f32[2,4,32,256]{3,2,1,0:T(8,128)} %get-tuple-element.170), channel_id=1, source_target_pairs={{0,1},{8,15},{16,17},{24,31},{2,3},{10,13},{18,19},{26,29},{4,5},{... | collective-permute-start | bytes 786440 | tf_op jit(solution)/shard_map/ppermute | solution.py:52
  62.6 13.1 %collective-permute-start.95 = (f32[2,4,32,256]{3,2,1,0:T(8,128)}, f32[2,4,32,256]{3,2,1,0:T(8,128)S(1)}, u32[]{:S(2)}, u32[]{:S(2)}) collective-permute-start(f32[2,4,32,256]{3,2,1,0:T(8,128)} %get-tuple-element.171), channel_id=1, source_target_pairs={{0,65},{8,79},{16,81},{24,95},{2,67},{10,77},{18,83},{26,93},{4,69... | collective-permute-start | bytes 786440 | tf_op jit(solution)/shard_map/ppermute | solution.py:52
  76.3 24.3 %collective-permute-start.96 = (f32[2,2,4,32,256]{4,3,2,1,0:T(8,128)S(1)}, f32[2,2,4,32,256]{4,3,2,1,0:T(8,128)S(1)}, u32[]{:S(2)}, u32[]{:S(2)}) collective-permute-start(f32[2,2,4,32,256]{4,3,2,1,0:T(8,128)S(1)} %shard_map.131.own), channel_id=1, source_target_pairs={{0,32},{8,40},{16,48},{24,56},{2,34},{10,42},{18,50},{26,58},{4,36... | collective-permute-start | bytes 1572872 | tf_op jit(solution)/shard_map/ppermute | solution.py:52
  79.1 25.7 %collective-permute-start.90 = (f32[2,4,32,256]{3,2,1,0:T(8,128)S(1)}, f32[2,4,32,256]{3,2,1,0:T(8,128)S(1)}, u32[]{:S(2)}, u32[]{:S(2)}) collective-permute-start(f32[2,4,32,256]{3,2,1,0:T(8,128)S(1)} %get-tuple-element.165.hi.hi_b), channel_id=1, source_target_pairs={{0,2},{8,16},{16,18},{24,0},{2,4},{10,8},{18,20},{26,24},{4,6},{12... | collective-permute-start | bytes 786440 | tf_op jit(solution)/shard_map/ppermute | solution.py:52
  87.8 17.0 %collective-permute-start.91 = (f32[2,4,32,256]{3,2,1,0:T(8,128)S(1)}, f32[2,4,32,256]{3,2,1,0:T(8,128)S(1)}, u32[]{:S(2)}, u32[]{:S(2)}) collective-permute-start(f32[2,4,32,256]{3,2,1,0:T(8,128)S(1)} %get-tuple-element.164.lo.lo_b), channel_id=1, source_target_pairs={{0,24},{8,10},{16,8},{24,26},{2,0},{10,12},{18,16},{26,28},{4,2},{... | collective-permute-start | bytes 786440 | tf_op jit(solution)/shard_map/ppermute | solution.py:52
  108.4 8.5 %collective-permute-start.97 = (f32[2,4,32,256]{3,2,1,0:T(8,128)S(1)}, f32[2,4,32,256]{3,2,1,0:T(8,128)S(1)}, u32[]{:S(2)}, u32[]{:S(2)}) collective-permute-start(f32[2,4,32,256]{3,2,1,0:T(8,128)S(1)} %get-tuple-element.173.hi.hi_b), channel_id=1, source_target_pairs={{0,2},{8,16},{16,18},{24,0},{2,4},{10,8},{18,20},{26,24},{4,6},{12... | collective-permute-start | bytes 786440 | tf_op jit(solution)/shard_map/ppermute | solution.py:52
  108.5 8.5 %collective-permute-start.98 = (f32[2,4,32,256]{3,2,1,0:T(8,128)S(1)}, f32[2,4,32,256]{3,2,1,0:T(8,128)S(1)}, u32[]{:S(2)}, u32[]{:S(2)}) collective-permute-start(f32[2,4,32,256]{3,2,1,0:T(8,128)S(1)} %get-tuple-element.172.lo.lo_b), channel_id=1, source_target_pairs={{0,24},{8,10},{16,8},{24,26},{2,0},{10,12},{18,16},{26,28},{4,2},{... | collective-permute-start | bytes 786440 | tf_op jit(solution)/shard_map/ppermute | solution.py:52
  120.6 6.4 %collective-permute-start.100 = (f32[2,4,32,256]{3,2,1,0:T(8,128)S(1)}, f32[2,4,32,256]{3,2,1,0:T(8,128)S(1)}, u32[]{:S(2)}, u32[]{:S(2)}) collective-permute-start(f32[2,4,32,256]{3,2,1,0:T(8,128)S(1)} %get-tuple-element.174.lo.lo_b), channel_id=1, source_target_pairs={{0,24},{8,10},{16,8},{24,26},{2,0},{10,12},{18,16},{26,28},{4,2},{... | collective-permute-start | bytes 786440 | tf_op jit(solution)/shard_map/ppermute | solution.py:52
  123.0 7.0 %collective-permute-start.99 = (f32[2,4,32,256]{3,2,1,0:T(8,128)S(1)}, f32[2,4,32,256]{3,2,1,0:T(8,128)S(1)}, u32[]{:S(2)}, u32[]{:S(2)}) collective-permute-start(f32[2,4,32,256]{3,2,1,0:T(8,128)S(1)} %get-tuple-element.175.hi.hi_b), channel_id=1, source_target_pairs={{0,2},{8,16},{16,18},{24,0},{2,4},{10,8},{18,20},{26,24},{4,6},{12... | collective-permute-start | bytes 786440 | tf_op jit(solution)/shard_map/ppermute | solution.py:52
  123.0 17.0 %collective-permute-start.103 = (f32[2,2,4,32,256]{4,3,2,1,0:T(8,128)S(1)}, f32[2,2,4,32,256]{4,3,2,1,0:T(8,128)S(1)}, u32[]{:S(2)}, u32[]{:S(2)}) collective-permute-start(f32[2,2,4,32,256]{4,3,2,1,0:T(8,128)S(1)} %get-tuple-element.178), channel_id=1, source_target_pairs={{0,32},{8,40},{16,48},{24,56},{2,34},{10,42},{18,50},{26,58},{4,36... | collective-permute-start | bytes 1572872 | tf_op jit(solution)/shard_map/ppermute | solution.py:52
  133.5 6.5 %collective-permute-start.101 = (f32[2,4,32,256]{3,2,1,0:T(8,128)S(1)}, f32[2,4,32,256]{3,2,1,0:T(8,128)S(1)}, u32[]{:S(2)}, u32[]{:S(2)}) collective-permute-start(f32[2,4,32,256]{3,2,1,0:T(8,128)S(1)} %get-tuple-element.177.hi), channel_id=1, source_target_pairs={{0,2},{8,16},{16,18},{24,0},{2,4},{10,8},{18,20},{26,24},{4,6},{12... | collective-permute-start | bytes 786440 | tf_op jit(solution)/shard_map/ppermute | solution.py:52
  133.6 6.4 %collective-permute-start.102 = (f32[2,4,32,256]{3,2,1,0:T(8,128)S(1)}, f32[2,4,32,256]{3,2,1,0:T(8,128)S(1)}, u32[]{:S(2)}, u32[]{:S(2)}) collective-permute-start(f32[2,4,32,256]{3,2,1,0:T(8,128)S(1)} %get-tuple-element.176.lo), channel_id=1, source_target_pairs={{0,24},{8,10},{16,8},{24,26},{2,0},{10,12},{18,16},{26,28},{4,2},{... | collective-permute-start | bytes 786440 | tf_op jit(solution)/shard_map/ppermute | solution.py:52
  143.6 5.2 %collective-permute-start.104 = (f32[2,4,16,256]{3,2,1,0:T(8,128)S(1)}, f32[2,4,16,256]{3,2,1,0:T(8,128)S(1)}, u32[]{:S(2)}, u32[]{:S(2)}) collective-permute-start(f32[2,4,16,256]{3,2,1,0:T(8,128)S(1)} %get-tuple-element.180), channel_id=1, source_target_pairs={{0,32},{8,40},{16,48},{24,56},{2,34},{10,42},{18,50},{26,58},{4,36... | collective-permute-start | bytes 393224 | tf_op jit(solution)/shard_map/ppermute | solution.py:52
  149.4 4.4 %collective-permute-start.105 = (f32[4,16,256]{2,1,0:T(8,128)S(1)}, f32[4,16,256]{2,1,0:T(8,128)S(1)}, u32[]{:S(2)}, u32[]{:S(2)}) collective-permute-start(f32[4,16,256]{2,1,0:T(8,128)S(1)} %get-tuple-element.181.kept), channel_id=1, source_target_pairs={{0,6},{8,14},{16,22},{24,30},{2,4},{10,12},{18,20},{26,28},{4,2},{... | collective-permute-start | bytes 196616 | tf_op jit(solution)/shard_map/ppermute | solution.py:52
  149.5 6.3 %collective-permute-start.106 = (f32[4,16,256]{2,1,0:T(8,128)S(1)}, f32[4,16,256]{2,1,0:T(8,128)S(1)}, u32[]{:S(2)}, u32[]{:S(2)}) collective-permute-start(f32[4,16,256]{2,1,0:T(8,128)S(1)} %get-tuple-element.182), channel_id=1, source_target_pairs={{0,64},{8,78},{16,80},{24,94},{2,66},{10,76},{18,82},{26,92},{4,68... | collective-permute-start | bytes 196616 | tf_op jit(solution)/shard_map/ppermute | solution.py:52
  149.6 6.3 %collective-permute-start.107 = (f32[4,16,256]{2,1,0:T(8,128)S(1)}, f32[4,16,256]{2,1,0:T(8,128)S(1)}, u32[]{:S(2)}, u32[]{:S(2)}) collective-permute-start(f32[4,16,256]{2,1,0:T(8,128)S(1)} %get-tuple-element.183), channel_id=1, source_target_pairs={{0,1},{8,15},{16,17},{24,31},{2,3},{10,13},{18,19},{26,29},{4,5},{... | collective-permute-start | bytes 196616 | tf_op jit(solution)/shard_map/ppermute | solution.py:52
  150.7 5.1 %collective-permute-start.108 = (f32[4,16,256]{2,1,0:T(8,128)S(1)}, f32[4,16,256]{2,1,0:T(8,128)S(1)}, u32[]{:S(2)}, u32[]{:S(2)}) collective-permute-start(f32[4,16,256]{2,1,0:T(8,128)S(1)} %get-tuple-element.184), channel_id=1, source_target_pairs={{0,65},{8,79},{16,81},{24,95},{2,67},{10,77},{18,83},{26,93},{4,69... | collective-permute-start | bytes 196616 | tf_op jit(solution)/shard_map/ppermute | solution.py:52
  156.5 22.6 %collective-permute-start.109 = (f32[2,4,16,256]{3,2,1,0:T(8,128)S(1)}, f32[2,4,16,256]{3,2,1,0:T(8,128)S(1)}, u32[]{:S(2)}, u32[]{:S(2)}) collective-permute-start(f32[2,4,16,256]{3,2,1,0:T(8,128)S(1)} %get-tuple-element.186.last), channel_id=1, source_target_pairs={{0,30},{8,6},{16,14},{24,22},{2,0},{10,8},{18,16},{26,24},{4,2},{1... | collective-permute-start | bytes 393224 | tf_op jit(solution)/shard_map/ppermute | solution.py:52
  171.7 5.6 %collective-permute-start.67 = (f32[2,4,16,256]{3,2,1,0:T(8,128)S(1)}, f32[2,4,16,256]{3,2,1,0:T(8,128)}, u32[]{:S(2)}, u32[]{:S(2)}) collective-permute-start(f32[2,4,16,256]{3,2,1,0:T(8,128)S(1)} %param.59), channel_id=1, source_target_pairs={{0,28},{8,4},{16,12},{24,20},{2,30},{10,6},{18,14},{26,22},{4,0},{... | collective-permute-start | bytes 393224 | tf_op jit(solution)/shard_map/cond/branch_27_fun/ppermute | solution.py:52
  171.8 7.3 %collective-permute-start.68 = (f32[2,4,16,256]{3,2,1,0:T(8,128)S(1)}, f32[2,4,16,256]{3,2,1,0:T(8,128)}, u32[]{:S(2)}, u32[]{:S(2)}) collective-permute-start(f32[2,4,16,256]{3,2,1,0:T(8,128)S(1)} %param.59), channel_id=1, source_target_pairs={{0,26},{8,2},{16,10},{24,18},{2,28},{10,4},{18,12},{26,20},{4,30},... | collective-permute-start | bytes 393224 | tf_op jit(solution)/shard_map/cond/branch_27_fun/ppermute | solution.py:52
  180.1 3.8 %collective-permute-start.110 = (f32[4,16,256]{2,1,0:T(8,128)S(1)}, f32[4,16,256]{2,1,0:T(8,128)S(1)}, u32[]{:S(2)}, u32[]{:S(2)}) collective-permute-start(f32[4,16,256]{2,1,0:T(8,128)S(1)} %get-tuple-element.191), channel_id=1, source_target_pairs={{0,32},{8,40},{16,48},{24,56},{2,34},{10,42},{18,50},{26,58},{4,36... | collective-permute-start | bytes 196616 | tf_op jit(solution)/shard_map/ppermute | solution.py:52
where the time goes:
time: 189 us; the launch traced here: 185 us
  starting transfers between devices  68.1 us (36%)
  waiting for transfers between devices  54.9 us (29%)
  Pallas kernels  27.2 us (14%)
  loops' own time  18.6 us (10%)
  local copies, waits for them, and re-layouts  12.8 us (7%)
  other arithmetic  2.61 us (1%)
    ppermute x29, starting transfers between devices, send(): return lax.ppermute(value, AXES, pairs)  68.1 us
    ppermute x29, waiting for transfers between devices, send(): return lax.ppermute(value, AXES, pairs)  54.9 us
    another operation x1, loops' own time, local(): lax.switch(plan[FREE], [lambda v, r=r: turn_model(v, aper % 2, r) for r i...  11.3 us
    pallas_call x3, Pallas kernels, local(): call(step_kernel, 8, outs, [(2, 4 * TX, AY, AZ)])  10.8 us
    unnamed x28, local copies, waits for them, and re-layouts  10.7 us
    another operation x1, loops' own time, local(): lax.switch(plan[FREE], [lambda v, r=r: turn_image(v, r) for r in range(32...  7.33 us
  transfers between devices with their start and end apart: 29, of which 17 were waited for; matrix products, arithmetic and copies ran while one was open for 2% of the time, Pallas kernels for 4%

commit v1 on v0

--- a/solution.py
+++ b/solution.py
@@ -28,19 +28,6 @@
     return [(x, c, y, z) for x in range(4) for c in range(2) for y in range(4) for z in range(4)]
 
 
-def flipped(y, z):
-    return 3 - y if z % 2 else y
-
-
-def on_path(j):
-    j = j % 16
-    return flipped(j % 4, j // 4), j // 4
-
-
-def path_place(y, z):
-    return 4 * z + flipped(y, z)
-
-
 def pairs_of(rule):
     pairs = [(device(*d), device(*rule(*d))) for d in everyone()]
     assert sorted(t for _, t in pairs) == list(range(128))
@@ -56,39 +43,22 @@
     return pairs_of(lambda x, c, y, z: (x, 1 - c, y, z))
 
 
-def along_path(by):
-    def rule(x, c, y, z):
-        return (x, c) + on_path(path_place(y, z) + by)
-
-    return pairs_of(rule)
-
-
 def state_first():
     def rule(x, c, y, z):
-        hi = x // 2
-        t = {(0, 0): (0, 1), (0, 1): (1, 1), (1, 0): (0, 0), (1, 1): (1, 0)}[(hi, c)]
-        return (2 * t[0] + x % 2, t[1], flipped(y, z), z)
+        t = {(0, 0): (0, 1), (0, 1): (1, 1), (1, 0): (0, 0), (1, 1): (1, 0)}[(x // 2, c)]
+        return (2 * t[0] + x % 2, t[1], y, z)
 
     return pairs_of(rule)
 
 
 def state_second():
-    def rule(x, c, y, z):
-        hi = x // 2
-        if hi == c:
-            return (x, c, 3 - y, z)
-        return (2 * (1 - hi) + x % 2, 1 - c, flipped(y, z), z)
-
-    return pairs_of(rule)
+    return [
+        (device(x, c, y, z), device((x + 2) % 4, 1 - c, y, z)) for x, c, y, z in everyone() if x // 2 != c
+    ]
 
 
 def across(by):
-    def rule(x, c, y, z):
-        if by == 0:
-            return (x, c, 3 - y, z)
-        return ((x + by) % 4, c, flipped(y, z), z)
-
-    return pairs_of(rule)
+    return pairs_of(lambda x, c, y, z: ((x + by) % 4, c, y, z))
 
 
 def rolled(by_low, by_high):
@@ -156,7 +126,7 @@
     return second, first
 
 
-CORE, X_HI, BLOCK, FREE, STAYS, EVEN, KEEP, PARITY_LAST, PARITY_FREE = range(9)
+CORE, X_HI, BLOCK, STAYS, PARITY_LAST, PARITY_FREE = range(6)
 PARITY, ROLE_TO, SIDE, SOURCE, OWNER, ROLE_FROM = 12, 16, 20, 24, 28, 32
 
 
@@ -165,9 +135,7 @@
     core, x_lo, x_hi = shot & 1, shot >> 1, aper & 1
     x = 2 * x_hi + x_lo
     z, y = aper >> 3, (aper >> 1) & 3
-    even_z = 1 - (z & 1)
-    block = 4 * z + jnp.where(even_z == 1, y, 3 - y)
-    straight = 4 * z + y
+    block = 4 * z + y
     turns = [o & 31 for o in offsets]
 
     def of(values, g):
@@ -188,11 +156,11 @@
 
     def row_of(g):
         o = of(offsets, g)
-        return (o + 2 * straight + (x_hi ^ (o & 1))) >> 5
+        return (o + 2 * block + (x_hi ^ (o & 1))) >> 5
 
     def parity_before(g):
         o = of(offsets, g)
-        return ((o >> 5) + (2 * straight + x_hi < (o & 31)).astype(jnp.int32)) & 1
+        return ((o >> 5) + (2 * block + x_hi < (o & 31)).astype(jnp.int32)) & 1
 
     group = group_of(x)
     offset = of(offsets, group)
@@ -200,10 +168,7 @@
         CORE: core,
         X_HI: x_hi,
         BLOCK: block,
-        FREE: free_turn,
-        STAYS: (x_hi == core).astype(jnp.int32) * even_z,
-        EVEN: even_z,
-        KEEP: jnp.where(free_turn == 31, 1 - x_hi, jnp.where(free_turn == 1, x_hi, 0)),
+        STAYS: (x_hi == core).astype(jnp.int32),
         PARITY_LAST: parity_before(last),
         PARITY_FREE: parity_before(free),
     }
@@ -217,7 +182,7 @@
     for h in range(2):
         row = (offset + 2 * block + h) >> 5
         out[SOURCE + h] = (x - (2 * (h ^ (offset & 1)) + (row >> 1))) & 3
-    return out
+    return out, free_turn
 
 
 def fetch(which, choices, sems):
@@ -235,10 +200,12 @@
         pltpu.make_async_copy(a, out, sems.at[k]).wait()
 
 
-def plan_kernel(ids, offsets, velocity, epsilon, delta, angle, plan, own, other, sems):
-    values = plan_values(ids, [offsets[g] for g in range(4)])
+def plan_kernel(ids, offsets, velocity, epsilon, delta, angle, plan, turn_z, turn_y, own, other, sems):
+    values, free_turn = plan_values(ids, [offsets[g] for g in range(4)])
     for k, v in values.items():
         plan[k] = v
+    turn_z[0] = free_turn >> 3
+    turn_y[0] = free_turn & 7
     fetch(
         values[CORE] == 0,
         (
@@ -273,7 +240,7 @@
             free[f, i] = jnp.where(mine_free, a, b)
 
 
-def send_kernel(plan, own, came, last, last_came, free, free_came, kept, one, two, *outs):
+def send_kernel(plan, own, came, last, last_came, free_came, kept, one, two, *outs):
     first, stays = plan[CORE] == 0, plan[STAYS] == 1
     for t in range(2):
         lo, hi = outs[4 + 2 * t : 6 + 2 * t]
@@ -283,26 +250,24 @@
                 lo[p, i] = jnp.where(first, b, a)
                 hi[p, i] = jnp.where(first, a, b)
     high = plan[X_HI] == 1
-    keep = plan[KEEP] == 1
     mine = [plan[PARITY + by] == plan[CORE] for by in range(4)]
     role = [plan[ROLE_TO + by] for by in range(4)]
     for f in range(2):
         for i in range(TX):
             a, b = own[f, i], came[f, i]
             turned_last = jnp.where(high, last_came[f, i], last[f, i])
-            turned_free = jnp.where(keep, free[f, i], free_came[f, i])
+            turned_free = free_came[f, i]
             for by in range(4):
                 straight = jnp.where(mine[by], a, b)
                 turned = jnp.where(role[by] == 1, turned_last, turned_free)
                 outs[by][f, i] = jnp.where(role[by] == 0, straight, turned)
 
 
-def tiles_kernel(plan, kept, got_0, got_1, got_2, got_3, out):
-    even = plan[EVEN] == 1
+def tiles_kernel(plan, kept, got_1, got_2, got_3, out):
     source = [plan[SOURCE + h] for h in range(2)]
     for f in range(2):
         for i in range(TX):
-            rows = [jnp.where(even, kept[f, i], got_0[f, i]), got_1[f, i], got_2[f, i], got_3[f, i]]
+            rows = [kept[f, i], got_1[f, i], got_2[f, i], got_3[f, i]]
             for h in range(2):
                 a = jnp.where(source[h] == 0, rows[0], rows[1])
                 b = jnp.where(source[h] == 2, rows[2], rows[3])
@@ -389,10 +354,9 @@
             outs[by][i] = jnp.where(plan[SIDE + by] == 0, lo, hi)
 
 
-def owners_kernel(plan, kept, got_0, got_1, got_2, got_3, straight, last, free):
-    even = plan[EVEN] == 1
+def owners_kernel(plan, kept, got_1, got_2, got_3, straight, last, free):
     for i in range(TX):
-        parts = [jnp.where(even, kept[i], got_0[i]), got_1[i], got_2[i], got_3[i]]
+        parts = [kept[i], got_1[i], got_2[i], got_3[i]]
         for k, out in enumerate((straight, last, free)):
             for core in range(2):
                 acc = jnp.zeros_like(parts[0])
@@ -402,14 +366,13 @@
                 out[core, i] = acc
 
 
-def image_kernel(plan, straight, last, last_came, free_low, free_high, keep, give):
+def image_kernel(plan, straight, last, last_came, free_came, keep, give):
     high, first = plan[X_HI] == 1, plan[CORE] == 0
     for i in range(TX):
         sums = []
         for core in range(2):
             turned = jnp.where(high, last_came[core, i], last[core, i])
-            free = jnp.where(high, free_high[core, i], free_low[core, i])
-            sums.append(straight[core, i] + turned + free)
+            sums.append(straight[core, i] + turned + free_came[core, i])
         keep[i] = jnp.where(first, sums[0], sums[1])
         give[i] = jnp.where(first, sums[1], sums[0])
 
@@ -478,8 +441,8 @@
         lax.fori_loop(0, TX, tile, 0)
 
 
-ANY = pl.BlockSpec(memory_space=pl.ANY)
-LIMIT = pltpu.CompilerParams(vmem_limit_bytes=32 * 1024 * 1024)
+HBM = pl.BlockSpec(memory_space=pltpu.HBM)
+LIMIT = pltpu.CompilerParams(vmem_limit_bytes=8 * 1024 * 1024)
 
 
 def call(kernel, n_in, outs, scratch=()):
@@ -497,27 +460,19 @@
 PART = (TX, HALF_Y, AZ)
 
 
-def roll(value, by, avoid):
-    by = by % 16
-    if by == 0:
-        return value
-    if by == avoid:
-        return roll(roll(value, 8, avoid), by - 8, avoid)
-    return send(value, rolled(by, by))
-
-
-def turn_model(value, x_hi, r):
-    low, high = -((r + 1) // 2), -(r // 2)
-    if r in (0, 1, 31) or r % 2 == 0:
-        return roll(value, high if r != 1 else low, 1)
-    if r in (3, 5, 27, 29):
-        return jnp.where(x_hi == 1, roll(value, high, 1), roll(value, low, 1))
-    return send(value, rolled(low, high))
-
-
-def turn_image(value, r):
-    low = roll(value, (r + 1) // 2, 15)
-    return low, low if r % 2 == 0 else roll(value, r // 2, 15)
+def turn(value, x_hi, turn_z, turn_y, sign):
+    def roll(v, by):
+        return send(v, rolled(sign * by, sign * by)) if by else v
+
+    def columns(v, r):
+        if r == 1:
+            return jnp.where(x_hi == 1, v, roll(v, 1))
+        if r % 2 == 0:
+            return roll(v, r // 2)
+        return send(v, rolled(sign * (r // 2 + 1), sign * (r // 2)))
+
+    value = lax.switch(turn_z[0], [lambda v, k=k: roll(v, 4 * k) for k in range(4)], value)
+    return lax.switch(turn_y[0], [lambda v, r=r: columns(v, r) for r in range(8)], value)
 
 
 def local(
@@ -537,13 +492,13 @@
 ):
     shot, aper = lax.axis_index("shot"), lax.axis_index("aper")
     ids = jnp.stack([shot, aper]).astype(jnp.int32)
-    swap, up, down = other_core(), along_path(1), along_path(-1)
-
-    plan, own, other = pl.pallas_call(
+    swap, up, down = other_core(), rolled(1, 1), rolled(-1, -1)
+
+    plan, turn_z, turn_y, own, other = pl.pallas_call(
         plan_kernel,
-        out_shape=[jax.ShapeDtypeStruct((40,), jnp.int32)] + [jax.ShapeDtypeStruct(TILE, F32)] * 2,
-        in_specs=[SMEM] * 2 + [ANY] * 4,
-        out_specs=[SMEM, VMEM, VMEM],
+        out_shape=[jax.ShapeDtypeStruct((n,), jnp.int32) for n in (40, 1, 1)] + [jax.ShapeDtypeStruct(TILE, F32)] * 2,
+        in_specs=[SMEM] * 2 + [HBM] * 4,
+        out_specs=[SMEM] * 3 + [VMEM] * 2,
         scratch_shapes=[pltpu.SemaphoreType.DMA((4,))],
         compiler_params=LIMIT,
     )(ids, offsets, velocity, thomsen_epsilon, thomsen_delta, tilt_angle)
@@ -551,7 +506,7 @@
     one, two = pl.pallas_call(
         state_kernel,
         out_shape=[jax.ShapeDtypeStruct((2,) + TILE, F32)] * 2,
-        in_specs=[SMEM] + [ANY] * 4,
+        in_specs=[SMEM] + [HBM] * 4,
         out_specs=[VMEM] * 2,
         scratch_shapes=[pltpu.SemaphoreType.DMA((4,))],
         compiler_params=LIMIT,
@@ -559,15 +514,13 @@
     got_one, got_two = send(one, state_first()), send(two, state_second())
 
     last, free = call(rows_kernel, 2, [TILE] * 2)(plan, own, came)
-    last_came = send(last, rolled(1, 1))
-    free_came = lax.switch(
-        plan[FREE], [lambda v, r=r: turn_model(v, aper % 2, r) for r in range(32)], free
+    last_came = send(last, up)
+    free_came = turn(free, aper % 2, turn_z, turn_y, -1)
+    *rows, lo, hi, lo_b, hi_b = call(send_kernel, 8, [TILE] * 8)(
+        plan, own, came, last, last_came, free_came, two, got_one, got_two
     )
-    *rows, lo, hi, lo_b, hi_b = call(send_kernel, 9, [TILE] * 8)(
-        plan, own, came, last, last_came, free, free_came, two, got_one, got_two
-    )
-    got = [send(rows[by], across(by)) for by in range(4)]
-    tiles = call(tiles_kernel, 5, [(2,) + TILE])(plan, rows[0], *got)[0]
+    got = [send(rows[by], across(by)) for by in range(1, 4)]
+    tiles = call(tiles_kernel, 4, [(2,) + TILE])(plan, rows[0], *got)[0]
     coef = call(coef_kernel, 2, [(6, 8, AY, AZ)])(plan, tiles, send(tiles, swap))[0]
 
     n_rec = receiver_cell.shape[1]
@@ -597,11 +550,11 @@
     )(plan, lo, hi, lo_b, hi_b, low, high, coef, inj[STEPS - 1], shared)
 
     parts = call(total_kernel, 2, [PART] * 4)(plan, keep, send(give, swap))
-    got = [send(parts[by], across(by)) for by in range(4)]
-    straight, last, free = call(owners_kernel, 5, [(2,) + PART] * 3)(plan, parts[0], *got)
-    last_came = send(last, rolled(15, 15))
-    free_low, free_high = lax.switch(plan[FREE], [lambda v, r=r: turn_image(v, r) for r in range(32)], free)
-    keep, give = call(image_kernel, 5, [PART] * 2)(plan, straight, last, last_came, free_low, free_high)
+    got = [send(parts[by], across(by)) for by in range(1, 4)]
+    straight, last, free = call(owners_kernel, 4, [(2,) + PART] * 3)(plan, parts[0], *got)
+    last_came = send(last, down)
+    free_came = turn(free, aper % 2, turn_z, turn_y, 1)
+    keep, give = call(image_kernel, 4, [PART] * 2)(plan, straight, last, last_came, free_came)
     return call(join_kernel, 2, [(TX, AY, AZ)])(plan, keep, send(give, swap))[0]
 
 

time: 189 us -> 141 us (0.75); the launches traced: 185 us -> 142 us
  loops' own time: 18.6 us -> 0.09 us
  starting transfers between devices: 68.1 us -> 56 us
  waiting for transfers between devices: 54.9 us -> 45 us
    another operation x2 -> x4, loops' own time: 18.6 us -> 0.09 us  [the longest x2 0.06 us: turn(): lax.switch(turn_y[0], [lambda v, r=r: columns(v, r) for r in range(8)], v...]
    ppermute x29 -> x25, starting transfers between devices: 68.1 us -> 56 us  [send(): return lax.ppermute(value, AXES, pairs)]
    ppermute x29 -> x25, waiting for transfers between devices: 54.9 us -> 45 us  [send(): return lax.ppermute(value, AXES, pairs)]
    unnamed x28 -> x30, local copies, waits for them, and re-layouts: 10.7 us -> 11.1 us
  transfers between devices with their start and end apart: 29 -> 25, of which waited for: 17 -> 14; matrix products, arithmetic and copies ran while one was open for 2% -> 2% of each run, Pallas kernels for 4% -> 5%
where the time goes in v1:
time: 141 us; the launch traced here: 142 us
  starting transfers between devices  56 us (40%)
  waiting for transfers between devices  45 us (32%)
  Pallas kernels  25.6 us (18%)
  local copies, waits for them, and re-layouts  12.6 us (9%)
  between operations  1.55 us (1%)
    ppermute x25, starting transfers between devices, send(): return lax.ppermute(value, AXES, pairs)  56 us
    ppermute x25, waiting for transfers between devices, send(): return lax.ppermute(value, AXES, pairs)  45 us
    unnamed x30, local copies, waits for them, and re-layouts  11.1 us
    pallas_call x3, Pallas kernels, local(): call(step_kernel, 8, outs, [(2, 4 * TX, AY, AZ)])  10.5 us
    pallas_call x1, Pallas kernels, local(): call(last_kernel, 9, [(2,) + PART] * 2, [(2, 4 * TX, AY, AZ), (2, TX, AY,...  3.52 us
  transfers between devices with their start and end apart: 25, of which 14 were waited for; matrix products, arithmetic and copies ran while one was open for 2% of the time, Pallas kernels for 5%

profile of v1, /device:TPU:1, one launch (start us, length us, event | category | flops | bytes accessed | tf_op | source)
XLA Modules:
  0.0 141.7 jit_solution(11109593538019075762)
XLA Ops:
  0.1 0.9 copy-done.9
  1.0 0.9 copy-done.10
  1.9 0.9 copy-done.11
  2.8 0.9 copy-done.12
  3.7 0.7 copy-done.13
  4.4 2.1 %shard_map.127 = (s32[40]{0:T(128)S(1)}, s32[1]{0:T(128)}, s32[1]{0:T(128)}, f32[2,4,32,256]{3,2,1,0:T(8,128)S(1)}, f32[2,4,32,256]{3,2,1,0:T(8,128)S(1)}) custom-call(s32[2]{0:T(128)S(1)} %pad_add_fusion.ids, s32[4]{0:T(128)S(1)} %copy-done.13, f32[4,32,256]{2,1,0:T(8,128)S(1)} %copy-done.9, f32[4,32,256]{2,1,0:T(8,128)S(1)} %copy-done.10, ...), custom_call_target="tpu_custom_call" | custom-call | tf_op jit(solution)/shard_map/pallas_call | solution.py:497
  6.5 1.5 %collective-permute-start.20 = (f32[2,4,32,256]{3,2,1,0:T(8,128)S(1)}, f32[2,4,32,256]{3,2,1,0:T(8,128)S(1)}, u32[]{:S(2)}, u32[]{:S(2)}) collective-permute-start(f32[2,4,32,256]{3,2,1,0:T(8,128)S(1)} %get-tuple-element.104), channel_id=1, source_target_pairs={{0,32},{8,40},{16,48},{24,56},{2,34},{10,42},{18,50},{26,58},{4,36... | collective-permute-start | bytes 786440 | tf_op jit(solution)/shard_map/ppermute | solution.py:39
  8.0 0.9 copy-done.3
  8.9 0.9 copy-done.4
  9.9 0.9 copy-done.5
  10.8 0.9 copy-done.6
  11.8 0.7 shard_map.129
  12.4 4.6 %collective-permute-start.23 = (f32[2,2,4,32,256]{4,3,2,1,0:T(8,128)S(1)}, f32[2,2,4,32,256]{4,3,2,1,0:T(8,128)S(1)}, u32[]{:S(2)}, u32[]{:S(2)}) collective-permute-start(f32[2,2,4,32,256]{4,3,2,1,0:T(8,128)S(1)} %get-tuple-element.109.kept), channel_id=1, source_target_pairs={{32,1},{40,9},{48,17},{56,25},{34,3},{42,11},{50,19},{58,27},{36,5... | collective-permute-start | bytes 1572872 | tf_op jit(solution)/shard_map/ppermute | solution.py:39
  17.2 0.6 shard_map.128
  17.8 1.4 collective-permute-start.21
  20.5 12.9 %conditional.5 = (f32[2,4,32,256]{3,2,1,0:T(8,128)S(1)}) conditional(s32[]{:T(128)} %bitcast.2, f32[2,4,32,256]{3,2,1,0:T(8,128)S(1)} %get-tuple-element.141, (s32[]{:T(128)}, f32[2,4,32,256]{3,2,1,0:T(8,128)S(1)}) %tuple.77, f32[2,4,32,256]{3,2,1,0:T(8,128)S(1)} %get-tuple-element.141, ...), branch_computations={%region_4.5_spmd, %region_5.6_spmd, %region_6.7_spmd, %region_7.8_... | conditional | flops 65537 | bytes 1835066 | solution.py:475
  20.5 6.2 %collective-permute-start.5 = (f32[2,4,32,256]{3,2,1,0:T(8,128)S(1)}, f32[2,4,32,256]{3,2,1,0:T(8,128)S(1)}, u32[]{:S(2)}, u32[]{:S(2)}) collective-permute-start(f32[2,4,32,256]{3,2,1,0:T(8,128)S(1)} %param.8), channel_id=1, source_target_pairs={{0,28},{8,4},{16,12},{24,20},{2,30},{10,6},{18,14},{26,22},{4,0},{... | collective-permute-start | bytes 786440 | tf_op jit(solution)/shard_map/cond/branch_4_fun/ppermute | solution.py:39
  26.7 6.7 %collective-permute-done.5 = f32[2,4,32,256]{3,2,1,0:T(8,128)S(1)} collective-permute-done((f32[2,4,32,256]{3,2,1,0:T(8,128)S(1)}, f32[2,4,32,256]{3,2,1,0:T(8,128)S(1)}, u32[]{:S(2)}, u32[]{:S(2)}) %collective-permute-start.5) | collective-permute-done | bytes 262176 | tf_op jit(solution)/shard_map/cond/branch_4_fun/ppermute | solution.py:39
  33.4 0.7 copy-done.14
  34.1 2.0 %shard_map.130 = (f32[2,4,32,256]{3,2,1,0:T(8,128)S(1)}, f32[2,4,32,256]{3,2,1,0:T(8,128)}, f32[2,4,32,256]{3,2,1,0:T(8,128)}, f32[2,4,32,256]{3,2,1,0:T(8,128)}...) custom-call(s32[40]{0:T(128)S(1)} %get-tuple-element.102.plan, ...), custom_call_target="tpu_custom_call" | custom-call | tf_op jit(solution)/shard_map/pallas_call | solution.py:519
  36.1 0.7 copy-done.1
  36.8 0.7 copy-done.7
  37.5 0.3 collective-permute-start.26
  37.8 2.7 %collective-permute-start.27 = (f32[2,4,32,256]{3,2,1,0:T(8,128)}, f32[2,4,32,256]{3,2,1,0:T(8,128)S(1)}, u32[]{:S(2)}, u32[]{:S(2)}) collective-permute-start(f32[2,4,32,256]{3,2,1,0:T(8,128)} %get-tuple-element.117), channel_id=1, source_target_pairs={{0,1},{8,9},{16,17},{24,25},{2,3},{10,11},{18,19},{26,27},{4,5},{1... | collective-permute-start | bytes 786440 | tf_op jit(solution)/shard_map/ppermute | solution.py:39
  40.8 0.7 fusion
  41.6 3.8 %collective-permute-done.26.got_1 = f32[2,4,32,256]{3,2,1,0:T(8,128)S(1)} collective-permute-done((f32[2,4,32,256]{3,2,1,0:T(8,128)}, f32[2,4,32,256]{3,2,1,0:T(8,128)S(1)}, u32[]{:S(2)}, u32[]{:S(2)}) %collective-permute-start.26) | collective-permute-done | bytes 262176 | tf_op jit(solution)/shard_map/ppermute | solution.py:39
  45.3 6.5 %collective-permute-done.27.got_2 = f32[2,4,32,256]{3,2,1,0:T(8,128)S(1)} collective-permute-done((f32[2,4,32,256]{3,2,1,0:T(8,128)}, f32[2,4,32,256]{3,2,1,0:T(8,128)S(1)}, u32[]{:S(2)}, u32[]{:S(2)}) %collective-permute-start.27) | collective-permute-done | bytes 262176 | tf_op jit(solution)/shard_map/ppermute | solution.py:39
  51.9 0.6 collective-permute-done.28.got_3
  52.4 0.9 copy-done.8
  53.4 0.6 shard_map.131.own
  54.0 1.5 %collective-permute-start.29 = (f32[2,2,4,32,256]{4,3,2,1,0:T(8,128)S(1)}, f32[2,2,4,32,256]{4,3,2,1,0:T(8,128)S(1)}, u32[]{:S(2)}, u32[]{:S(2)}) collective-permute-start(f32[2,2,4,32,256]{4,3,2,1,0:T(8,128)S(1)} %shard_map.131.own), channel_id=1, source_target_pairs={{0,32},{8,40},{16,48},{24,56},{2,34},{10,42},{18,50},{26,58},{4,36... | collective-permute-start | bytes 1572872 | tf_op jit(solution)/shard_map/ppermute | solution.py:39
  55.5 0.7 fusion.1
  56.2 4.8 %collective-permute-start.25 = (f32[2,4,32,256]{3,2,1,0:T(8,128)S(1)}, f32[2,4,32,256]{3,2,1,0:T(8,128)S(1)}, u32[]{:S(2)}, u32[]{:S(2)}) collective-permute-start(f32[2,4,32,256]{3,2,1,0:T(8,128)S(1)} %get-tuple-element.111.lo.lo_b), channel_id=1, source_target_pairs={{0,30},{8,6},{16,14},{24,22},{2,0},{10,8},{18,16},{26,24},{4,2},{1... | collective-permute-start | bytes 786440 | tf_op jit(solution)/shard_map/ppermute | solution.py:39
  61.0 0.8 bitcast_select_fusion.1.amounts
  61.8 1.6 %shard_map.133 = f32[4,8,32,256]{3,2,1,0:T(8,128)S(1)} custom-call(s32[40]{0:T(128)S(1)} %get-tuple-element.102.plan, s32[3,256]{1,0:T(4,128)S(1)} %bitcast_select_fusion.cells, f32[4,256]{1,0:T(4,128)S(1)} %bitcast_select_fusion.1.amounts), custom_call_target="tpu_custom_call" | custom-call | tf_op jit(solution)/shard_map/pallas_call | solution.py:535
  63.5 1.0 shard_map.132.coef
  64.5 2.9 %collective-permute-done.24.low = f32[2,4,32,256]{3,2,1,0:T(8,128)S(1)} collective-permute-done((f32[2,4,32,256]{3,2,1,0:T(8,128)S(1)}, f32[2,4,32,256]{3,2,1,0:T(8,128)S(1)}, u32[]{:S(2)}, u32[]{:S(2)}) %collective-permute-start.24) | collective-permute-done | bytes 262176 | tf_op jit(solution)/shard_map/ppermute | solution.py:39
  67.5 3.5 %shard_map.134 = (f32[2,4,32,256]{3,2,1,0:T(8,128)S(1)}, f32[2,4,32,256]{3,2,1,0:T(8,128)S(1)}) custom-call(s32[40]{0:T(128)S(1)} %get-tuple-element.102.plan, f32[2,4,32,256]{3,2,1,0:T(8,128)S(1)} %get-tuple-element.111.lo.lo_b, f32[2,4,32,256]{3,2,1,0:T(8,128)S(1)} %get-tuple-element.112.hi.hi_b, f32[2,4,32,256]{3,2,1,0:T(8,128)S(1)} %get-tuple-element.113.lo_b, ...), custom_call_target="tpu_custom_call" | custom-call | tf_op jit(solution)/shard_map/pallas_call | solution.py:541
  71.1 4.8 %collective-permute-start.31 = (f32[2,4,32,256]{3,2,1,0:T(8,128)S(1)}, f32[2,4,32,256]{3,2,1,0:T(8,128)S(1)}, u32[]{:S(2)}, u32[]{:S(2)}) collective-permute-start(f32[2,4,32,256]{3,2,1,0:T(8,128)S(1)} %get-tuple-element.119.lo.lo_b), channel_id=1, source_target_pairs={{0,30},{8,6},{16,14},{24,22},{2,0},{10,8},{18,16},{26,24},{4,2},{1... | collective-permute-start | bytes 786440 | tf_op jit(solution)/shard_map/ppermute | solution.py:39
  75.8 5.6 %collective-permute-done.30.low = f32[2,4,32,256]{3,2,1,0:T(8,128)S(1)} collective-permute-done((f32[2,4,32,256]{3,2,1,0:T(8,128)S(1)}, f32[2,4,32,256]{3,2,1,0:T(8,128)S(1)}, u32[]{:S(2)}, u32[]{:S(2)}) %collective-permute-start.30) | collective-permute-done | bytes 262176 | tf_op jit(solution)/shard_map/ppermute | solution.py:39
  81.4 3.5 %shard_map.135 = (f32[2,4,32,256]{3,2,1,0:T(8,128)S(1)}, f32[2,4,32,256]{3,2,1,0:T(8,128)S(1)}, f32[2,2,4,32,256]{4,3,2,1,0:T(8,128)S(1)}) custom-call(s32[40]{0:T(128)S(1)} %get-tuple-element.102.plan, f32[2,4,32,256]{3,2,1,0:T(8,128)S(1)} %get-tuple-element.119.lo.lo_b, f32[2,4,32,256]{3,2,1,0:T(8,128)S(1)} %get-tuple-element.120.hi.hi_b, ...), custom_call_target="tpu_custom_call" | custom-call | tf_op jit(solution)/shard_map/pallas_call | solution.py:541
  85.0 4.8 %collective-permute-start.33 = (f32[2,4,32,256]{3,2,1,0:T(8,128)S(1)}, f32[2,4,32,256]{3,2,1,0:T(8,128)S(1)}, u32[]{:S(2)}, u32[]{:S(2)}) collective-permute-start(f32[2,4,32,256]{3,2,1,0:T(8,128)S(1)} %get-tuple-element.121.lo.lo_b), channel_id=1, source_target_pairs={{0,30},{8,6},{16,14},{24,22},{2,0},{10,8},{18,16},{26,24},{4,2},{1... | collective-permute-start | bytes 786440 | tf_op jit(solution)/shard_map/ppermute | solution.py:39
  89.8 2.2 %collective-permute-start.36 = (f32[2,2,4,32,256]{4,3,2,1,0:T(8,128)S(1)}, f32[2,2,4,32,256]{4,3,2,1,0:T(8,128)S(1)}, u32[]{:S(2)}, u32[]{:S(2)}) collective-permute-start(f32[2,2,4,32,256]{4,3,2,1,0:T(8,128)S(1)} %get-tuple-element.125), channel_id=1, source_target_pairs={{0,32},{8,40},{16,48},{24,56},{2,34},{10,42},{18,50},{26,58},{4,36... | collective-permute-start | bytes 1572872 | tf_op jit(solution)/shard_map/ppermute | solution.py:39
  92.0 2.4 %collective-permute-done.32.low = f32[2,4,32,256]{3,2,1,0:T(8,128)S(1)} collective-permute-done((f32[2,4,32,256]{3,2,1,0:T(8,128)S(1)}, f32[2,4,32,256]{3,2,1,0:T(8,128)S(1)}, u32[]{:S(2)}, u32[]{:S(2)}) %collective-permute-start.32) | collective-permute-done | bytes 262176 | tf_op jit(solution)/shard_map/ppermute | solution.py:39
  94.4 3.5 %shard_map.136 = (f32[2,4,32,256]{3,2,1,0:T(8,128)S(1)}, f32[2,4,32,256]{3,2,1,0:T(8,128)S(1)}) custom-call(s32[40]{0:T(128)S(1)} %get-tuple-element.102.plan, f32[2,4,32,256]{3,2,1,0:T(8,128)S(1)} %get-tuple-element.121.lo.lo_b, f32[2,4,32,256]{3,2,1,0:T(8,128)S(1)} %get-tuple-element.122.hi.hi_b, f32[2,4,32,256]{3,2,1,0:T(8,128)S(1)} %get-tuple-element.119.lo.lo_b, ...), custom_call_target="tpu_custom_call" | custom-call | tf_op jit(solution)/shard_map/pallas_call | solution.py:541
  98.0 4.8 %collective-permute-start.35 = (f32[2,4,32,256]{3,2,1,0:T(8,128)S(1)}, f32[2,4,32,256]{3,2,1,0:T(8,128)S(1)}, u32[]{:S(2)}, u32[]{:S(2)}) collective-permute-start(f32[2,4,32,256]{3,2,1,0:T(8,128)S(1)} %get-tuple-element.123.lo), channel_id=1, source_target_pairs={{0,30},{8,6},{16,14},{24,22},{2,0},{10,8},{18,16},{26,24},{4,2},{1... | collective-permute-start | bytes 786440 | tf_op jit(solution)/shard_map/ppermute | solution.py:39
  102.8 3.8 %collective-permute-done.34.low = f32[2,4,32,256]{3,2,1,0:T(8,128)S(1)} collective-permute-done((f32[2,4,32,256]{3,2,1,0:T(8,128)S(1)}, f32[2,4,32,256]{3,2,1,0:T(8,128)S(1)}, u32[]{:S(2)}, u32[]{:S(2)}) %collective-permute-start.34) | collective-permute-done | bytes 262176 | tf_op jit(solution)/shard_map/ppermute | solution.py:39
  106.5 3.5 %shard_map.137 = (f32[2,4,16,256]{3,2,1,0:T(8,128)S(1)}, f32[2,4,16,256]{3,2,1,0:T(8,128)S(1)}) custom-call(s32[40]{0:T(128)S(1)} %get-tuple-element.102.plan, f32[2,4,32,256]{3,2,1,0:T(8,128)S(1)} %get-tuple-element.123.lo, f32[2,4,32,256]{3,2,1,0:T(8,128)S(1)} %get-tuple-element.124.hi, f32[2,4,32,256]{3,2,1,0:T(8,128)S(1)} %get-tuple-element.121.lo.lo_b, ...), custom_call_target="tpu_custom_call" | custom-call | tf_op jit(solution)/shard_map/pallas_call | solution.py:548
  110.1 3.8 %collective-permute-start.37 = (f32[2,4,16,256]{3,2,1,0:T(8,128)S(1)}, f32[2,4,16,256]{3,2,1,0:T(8,128)S(1)}, u32[]{:S(2)}, u32[]{:S(2)}) collective-permute-start(f32[2,4,16,256]{3,2,1,0:T(8,128)S(1)} %get-tuple-element.127), channel_id=1, source_target_pairs={{0,32},{8,40},{16,48},{24,56},{2,34},{10,42},{18,50},{26,58},{4,36... | collective-permute-start | bytes 393224 | tf_op jit(solution)/shard_map/ppermute | solution.py:39
  113.9 1.0 collective-permute-done.37.came
  114.9 0.6 shard_map.138
  115.5 0.6 collective-permute-start.38
  116.1 3.0 %collective-permute-start.39 = (f32[4,16,256]{2,1,0:T(8,128)S(1)}, f32[4,16,256]{2,1,0:T(8,128)S(1)}, u32[]{:S(2)}, u32[]{:S(2)}) collective-permute-start(f32[4,16,256]{2,1,0:T(8,128)S(1)} %get-tuple-element.130), channel_id=1, source_target_pairs={{0,1},{8,9},{16,17},{24,25},{2,3},{10,11},{18,19},{26,27},{4,5},{1... | collective-permute-start | bytes 196616 | tf_op jit(solution)/shard_map/ppermute | solution.py:39
  119.1 0.8 collective-permute-done.38.got_1
  119.9 2.2 %collective-permute-done.39.got_2 = f32[4,16,256]{2,1,0:T(8,128)S(1)} collective-permute-done((f32[4,16,256]{2,1,0:T(8,128)S(1)}, f32[4,16,256]{2,1,0:T(8,128)S(1)}, u32[]{:S(2)}, u32[]{:S(2)}) %collective-permute-start.39) | collective-permute-done | bytes 65568 | tf_op jit(solution)/shard_map/ppermute | solution.py:39
  122.0 0.5 collective-permute-done.40.got_3
  122.5 0.7 shard_map.139
  123.2 5.1 %collective-permute-start.41 = (f32[2,4,16,256]{3,2,1,0:T(8,128)S(1)}, f32[2,4,16,256]{3,2,1,0:T(8,128)S(1)}, u32[]{:S(2)}, u32[]{:S(2)}) collective-permute-start(f32[2,4,16,256]{3,2,1,0:T(8,128)S(1)} %get-tuple-element.133.last), channel_id=1, source_target_pairs={{0,30},{8,6},{16,14},{24,22},{2,0},{10,8},{18,16},{26,24},{4,2},{1... | collective-permute-start | bytes 393224 | tf_op jit(solution)/shard_map/ppermute | solution.py:39
  128.3 7.5 %conditional.7 = (f32[2,4,16,256]{3,2,1,0:T(8,128)S(1)}) conditional(s32[]{:T(128)} %bitcast.2, f32[2,4,16,256]{3,2,1,0:T(8,128)S(1)} %get-tuple-element.143, (s32[]{:T(128)}, f32[2,4,16,256]{3,2,1,0:T(8,128)S(1)}) %tuple.78, f32[2,4,16,256]{3,2,1,0:T(8,128)S(1)} %get-tuple-element.143, ...), branch_computations={%region_16.17_spmd, %region_17.18_spmd, %region_18.19_spmd, %regio... | conditional | flops 32769 | bytes 917562 | solution.py:475
  128.3 7.4 %collective-permute-done.14 = f32[2,4,16,256]{3,2,1,0:T(8,128)S(1)} collective-permute-done((f32[2,4,16,256]{3,2,1,0:T(8,128)S(1)}, f32[2,4,16,256]{3,2,1,0:T(8,128)S(1)}, u32[]{:S(2)}, u32[]{:S(2)}) %collective-permute-start.14) | collective-permute-done | bytes 131104 | tf_op jit(solution)/shard_map/cond/branch_4_fun/ppermute | solution.py:39
  135.8 0.6 shard_map.140
  136.4 3.2 %collective-permute-start.42 = (f32[4,16,256]{2,1,0:T(8,128)S(1)}, f32[4,16,256]{2,1,0:T(8,128)S(1)}, u32[]{:S(2)}, u32[]{:S(2)}) collective-permute-start(f32[4,16,256]{2,1,0:T(8,128)S(1)} %get-tuple-element.136), channel_id=1, source_target_pairs={{0,32},{8,40},{16,48},{24,56},{2,34},{10,42},{18,50},{26,58},{4,36... | collective-permute-start | bytes 196616 | tf_op jit(solution)/shard_map/ppermute | solution.py:39
  139.6 0.9 collective-permute-done.42.came
  140.5 1.2 shard_map.141
  (45 shorter events, 0.9 us)
Async XLA Ops:
  0.0 20.4 %copy-start = (s32[4,256,3]{1,0,2:T(4,128)S(1)}, s32[4,256,3]{1,0,2:T(4,128)}, u32[]{:S(2)}) copy-start(s32[4,256,3]{1,0,2:T(4,128)} %param.49) | copy-start | bytes 36868
  0.1 0.9 copy-start.9
  1.0 0.9 copy-start.10
  1.9 0.9 copy-start.11
  2.8 0.9 copy-start.12
  3.7 0.7 copy-start.13
  6.5 10.7 %collective-permute-start.20 = (f32[2,4,32,256]{3,2,1,0:T(8,128)S(1)}, f32[2,4,32,256]{3,2,1,0:T(8,128)S(1)}, u32[]{:S(2)}, u32[]{:S(2)}) collective-permute-start(f32[2,4,32,256]{3,2,1,0:T(8,128)S(1)} %get-tuple-element.104), channel_id=1, source_target_pairs={{0,32},{8,40},{16,48},{24,56},{2,34},{10,42},{18,50},{26,58},{4,36... | collective-permute-start | bytes 786440 | tf_op jit(solution)/shard_map/ppermute | solution.py:39
  8.0 0.9 copy-start.3
  8.9 0.9 copy-start.4
  9.9 0.9 copy-start.5
  10.8 0.9 copy-start.6
  12.4 21.0 %collective-permute-start.23 = (f32[2,2,4,32,256]{4,3,2,1,0:T(8,128)S(1)}, f32[2,2,4,32,256]{4,3,2,1,0:T(8,128)S(1)}, u32[]{:S(2)}, u32[]{:S(2)}) collective-permute-start(f32[2,2,4,32,256]{4,3,2,1,0:T(8,128)S(1)} %get-tuple-element.109.kept), channel_id=1, source_target_pairs={{32,1},{40,9},{48,17},{56,25},{34,3},{42,11},{50,19},{58,27},{36,5... | collective-permute-start | bytes 1572872 | tf_op jit(solution)/shard_map/ppermute | solution.py:39
  17.1 17.0 %collective-permute-start.22 = (f32[2,2,4,32,256]{4,3,2,1,0:T(8,128)S(1)}, f32[2,2,4,32,256]{4,3,2,1,0:T(8,128)S(1)}, u32[]{:S(2)}, u32[]{:S(2)}) collective-permute-start(f32[2,2,4,32,256]{4,3,2,1,0:T(8,128)S(1)} %get-tuple-element.110), channel_id=1, source_target_pairs={{0,32},{8,40},{16,48},{24,56},{2,34},{10,42},{18,50},{26,58},{4,36... | collective-permute-start | bytes 1572872 | tf_op jit(solution)/shard_map/ppermute | solution.py:39
  17.8 15.6 %collective-permute-start.21 = (f32[2,4,32,256]{3,2,1,0:T(8,128)S(1)}, f32[2,4,32,256]{3,2,1,0:T(8,128)S(1)}, u32[]{:S(2)}, u32[]{:S(2)}) collective-permute-start(f32[2,4,32,256]{3,2,1,0:T(8,128)S(1)} %get-tuple-element.105.last), channel_id=1, source_target_pairs={{0,2},{8,10},{16,18},{24,26},{2,4},{10,12},{18,20},{26,28},{4,6},{... | collective-permute-start | bytes 786440 | tf_op jit(solution)/shard_map/ppermute | solution.py:39
  20.5 12.8 %collective-permute-start.5 = (f32[2,4,32,256]{3,2,1,0:T(8,128)S(1)}, f32[2,4,32,256]{3,2,1,0:T(8,128)S(1)}, u32[]{:S(2)}, u32[]{:S(2)}) collective-permute-start(f32[2,4,32,256]{3,2,1,0:T(8,128)S(1)} %param.8), channel_id=1, source_target_pairs={{0,28},{8,4},{16,12},{24,20},{2,30},{10,6},{18,14},{26,22},{4,0},{... | collective-permute-start | bytes 786440 | tf_op jit(solution)/shard_map/cond/branch_4_fun/ppermute | solution.py:39
  33.4 0.7 copy-start.14
  36.1 0.7 copy-start.1
  36.8 0.7 copy-start.7
  37.5 7.8 %collective-permute-start.26 = (f32[2,4,32,256]{3,2,1,0:T(8,128)}, f32[2,4,32,256]{3,2,1,0:T(8,128)S(1)}, u32[]{:S(2)}, u32[]{:S(2)}) collective-permute-start(f32[2,4,32,256]{3,2,1,0:T(8,128)} %get-tuple-element.116), channel_id=1, source_target_pairs={{0,64},{8,72},{16,80},{24,88},{2,66},{10,74},{18,82},{26,90},{4,68... | collective-permute-start | bytes 786440 | tf_op jit(solution)/shard_map/ppermute | solution.py:39
  37.8 14.1 %collective-permute-start.27 = (f32[2,4,32,256]{3,2,1,0:T(8,128)}, f32[2,4,32,256]{3,2,1,0:T(8,128)S(1)}, u32[]{:S(2)}, u32[]{:S(2)}) collective-permute-start(f32[2,4,32,256]{3,2,1,0:T(8,128)} %get-tuple-element.117), channel_id=1, source_target_pairs={{0,1},{8,9},{16,17},{24,25},{2,3},{10,11},{18,19},{26,27},{4,5},{1... | collective-permute-start | bytes 786440 | tf_op jit(solution)/shard_map/ppermute | solution.py:39
  40.5 11.9 %collective-permute-start.28 = (f32[2,4,32,256]{3,2,1,0:T(8,128)}, f32[2,4,32,256]{3,2,1,0:T(8,128)S(1)}, u32[]{:S(2)}, u32[]{:S(2)}) collective-permute-start(f32[2,4,32,256]{3,2,1,0:T(8,128)} %get-tuple-element.118), channel_id=1, source_target_pairs={{0,65},{8,73},{16,81},{24,89},{2,67},{10,75},{18,83},{26,91},{4,69... | collective-permute-start | bytes 786440 | tf_op jit(solution)/shard_map/ppermute | solution.py:39
  52.4 0.9 copy-start.8
  54.0 9.5 %collective-permute-start.29 = (f32[2,2,4,32,256]{4,3,2,1,0:T(8,128)S(1)}, f32[2,2,4,32,256]{4,3,2,1,0:T(8,128)S(1)}, u32[]{:S(2)}, u32[]{:S(2)}) collective-permute-start(f32[2,2,4,32,256]{4,3,2,1,0:T(8,128)S(1)} %shard_map.131.own), channel_id=1, source_target_pairs={{0,32},{8,40},{16,48},{24,56},{2,34},{10,42},{18,50},{26,58},{4,36... | collective-permute-start | bytes 1572872 | tf_op jit(solution)/shard_map/ppermute | solution.py:39
  56.2 11.2 %collective-permute-start.24 = (f32[2,4,32,256]{3,2,1,0:T(8,128)S(1)}, f32[2,4,32,256]{3,2,1,0:T(8,128)S(1)}, u32[]{:S(2)}, u32[]{:S(2)}) collective-permute-start(f32[2,4,32,256]{3,2,1,0:T(8,128)S(1)} %get-tuple-element.112.hi.hi_b), channel_id=1, source_target_pairs={{0,2},{8,10},{16,18},{24,26},{2,4},{10,12},{18,20},{26,28},{4,6},{... | collective-permute-start | bytes 786440 | tf_op jit(solution)/shard_map/ppermute | solution.py:39
  56.2 11.2 %collective-permute-start.25 = (f32[2,4,32,256]{3,2,1,0:T(8,128)S(1)}, f32[2,4,32,256]{3,2,1,0:T(8,128)S(1)}, u32[]{:S(2)}, u32[]{:S(2)}) collective-permute-start(f32[2,4,32,256]{3,2,1,0:T(8,128)S(1)} %get-tuple-element.111.lo.lo_b), channel_id=1, source_target_pairs={{0,30},{8,6},{16,14},{24,22},{2,0},{10,8},{18,16},{26,24},{4,2},{1... | collective-permute-start | bytes 786440 | tf_op jit(solution)/shard_map/ppermute | solution.py:39
  63.5 4.0 %copy-start.2 = (f32[2,4,32,256]{3,2,1,0:T(8,128)S(1)}, f32[2,4,32,256]{3,2,1,0:T(8,128)}, u32[]{:S(2)}) copy-start(f32[2,4,32,256]{3,2,1,0:T(8,128)} %copy-done.1) | copy-start | bytes 786436
  71.0 10.4 %collective-permute-start.30 = (f32[2,4,32,256]{3,2,1,0:T(8,128)S(1)}, f32[2,4,32,256]{3,2,1,0:T(8,128)S(1)}, u32[]{:S(2)}, u32[]{:S(2)}) collective-permute-start(f32[2,4,32,256]{3,2,1,0:T(8,128)S(1)} %get-tuple-element.120.hi.hi_b), channel_id=1, source_target_pairs={{0,2},{8,10},{16,18},{24,26},{2,4},{10,12},{18,20},{26,28},{4,6},{... | collective-permute-start | bytes 786440 | tf_op jit(solution)/shard_map/ppermute | solution.py:39
  71.1 10.3 %collective-permute-start.31 = (f32[2,4,32,256]{3,2,1,0:T(8,128)S(1)}, f32[2,4,32,256]{3,2,1,0:T(8,128)S(1)}, u32[]{:S(2)}, u32[]{:S(2)}) collective-permute-start(f32[2,4,32,256]{3,2,1,0:T(8,128)S(1)} %get-tuple-element.119.lo.lo_b), channel_id=1, source_target_pairs={{0,30},{8,6},{16,14},{24,22},{2,0},{10,8},{18,16},{26,24},{4,2},{1... | collective-permute-start | bytes 786440 | tf_op jit(solution)/shard_map/ppermute | solution.py:39
  84.9 9.5 %collective-permute-start.32 = (f32[2,4,32,256]{3,2,1,0:T(8,128)S(1)}, f32[2,4,32,256]{3,2,1,0:T(8,128)S(1)}, u32[]{:S(2)}, u32[]{:S(2)}) collective-permute-start(f32[2,4,32,256]{3,2,1,0:T(8,128)S(1)} %get-tuple-element.122.hi.hi_b), channel_id=1, source_target_pairs={{0,2},{8,10},{16,18},{24,26},{2,4},{10,12},{18,20},{26,28},{4,6},{... | collective-permute-start | bytes 786440 | tf_op jit(solution)/shard_map/ppermute | solution.py:39
  85.0 9.4 %collective-permute-start.33 = (f32[2,4,32,256]{3,2,1,0:T(8,128)S(1)}, f32[2,4,32,256]{3,2,1,0:T(8,128)S(1)}, u32[]{:S(2)}, u32[]{:S(2)}) collective-permute-start(f32[2,4,32,256]{3,2,1,0:T(8,128)S(1)} %get-tuple-element.121.lo.lo_b), channel_id=1, source_target_pairs={{0,30},{8,6},{16,14},{24,22},{2,0},{10,8},{18,16},{26,24},{4,2},{1... | collective-permute-start | bytes 786440 | tf_op jit(solution)/shard_map/ppermute | solution.py:39
  89.8 16.8 %collective-permute-start.36 = (f32[2,2,4,32,256]{4,3,2,1,0:T(8,128)S(1)}, f32[2,2,4,32,256]{4,3,2,1,0:T(8,128)S(1)}, u32[]{:S(2)}, u32[]{:S(2)}) collective-permute-start(f32[2,2,4,32,256]{4,3,2,1,0:T(8,128)S(1)} %get-tuple-element.125), channel_id=1, source_target_pairs={{0,32},{8,40},{16,48},{24,56},{2,34},{10,42},{18,50},{26,58},{4,36... | collective-permute-start | bytes 1572872 | tf_op jit(solution)/shard_map/ppermute | solution.py:39
  97.9 8.6 %collective-permute-start.34 = (f32[2,4,32,256]{3,2,1,0:T(8,128)S(1)}, f32[2,4,32,256]{3,2,1,0:T(8,128)S(1)}, u32[]{:S(2)}, u32[]{:S(2)}) collective-permute-start(f32[2,4,32,256]{3,2,1,0:T(8,128)S(1)} %get-tuple-element.124.hi), channel_id=1, source_target_pairs={{0,2},{8,10},{16,18},{24,26},{2,4},{10,12},{18,20},{26,28},{4,6},{... | collective-permute-start | bytes 786440 | tf_op jit(solution)/shard_map/ppermute | solution.py:39
  98.0 8.5 %collective-permute-start.35 = (f32[2,4,32,256]{3,2,1,0:T(8,128)S(1)}, f32[2,4,32,256]{3,2,1,0:T(8,128)S(1)}, u32[]{:S(2)}, u32[]{:S(2)}) collective-permute-start(f32[2,4,32,256]{3,2,1,0:T(8,128)S(1)} %get-tuple-element.123.lo), channel_id=1, source_target_pairs={{0,30},{8,6},{16,14},{24,22},{2,0},{10,8},{18,16},{26,24},{4,2},{1... | collective-permute-start | bytes 786440 | tf_op jit(solution)/shard_map/ppermute | solution.py:39
  110.1 4.8 %collective-permute-start.37 = (f32[2,4,16,256]{3,2,1,0:T(8,128)S(1)}, f32[2,4,16,256]{3,2,1,0:T(8,128)S(1)}, u32[]{:S(2)}, u32[]{:S(2)}) collective-permute-start(f32[2,4,16,256]{3,2,1,0:T(8,128)S(1)} %get-tuple-element.127), channel_id=1, source_target_pairs={{0,32},{8,40},{16,48},{24,56},{2,34},{10,42},{18,50},{26,58},{4,36... | collective-permute-start | bytes 393224 | tf_op jit(solution)/shard_map/ppermute | solution.py:39
  115.5 4.4 %collective-permute-start.38 = (f32[4,16,256]{2,1,0:T(8,128)S(1)}, f32[4,16,256]{2,1,0:T(8,128)S(1)}, u32[]{:S(2)}, u32[]{:S(2)}) collective-permute-start(f32[4,16,256]{2,1,0:T(8,128)S(1)} %get-tuple-element.129), channel_id=1, source_target_pairs={{0,64},{8,72},{16,80},{24,88},{2,66},{10,74},{18,82},{26,90},{4,68... | collective-permute-start | bytes 196616 | tf_op jit(solution)/shard_map/ppermute | solution.py:39
  116.1 5.9 %collective-permute-start.39 = (f32[4,16,256]{2,1,0:T(8,128)S(1)}, f32[4,16,256]{2,1,0:T(8,128)S(1)}, u32[]{:S(2)}, u32[]{:S(2)}) collective-permute-start(f32[4,16,256]{2,1,0:T(8,128)S(1)} %get-tuple-element.130), channel_id=1, source_target_pairs={{0,1},{8,9},{16,17},{24,25},{2,3},{10,11},{18,19},{26,27},{4,5},{1... | collective-permute-start | bytes 196616 | tf_op jit(solution)/shard_map/ppermute | solution.py:39
  119.1 3.5 %collective-permute-start.40 = (f32[4,16,256]{2,1,0:T(8,128)S(1)}, f32[4,16,256]{2,1,0:T(8,128)S(1)}, u32[]{:S(2)}, u32[]{:S(2)}) collective-permute-start(f32[4,16,256]{2,1,0:T(8,128)S(1)} %get-tuple-element.131), channel_id=1, source_target_pairs={{0,65},{8,73},{16,81},{24,89},{2,67},{10,75},{18,83},{26,91},{4,69... | collective-permute-start | bytes 196616 | tf_op jit(solution)/shard_map/ppermute | solution.py:39
  123.2 12.6 %collective-permute-start.41 = (f32[2,4,16,256]{3,2,1,0:T(8,128)S(1)}, f32[2,4,16,256]{3,2,1,0:T(8,128)S(1)}, u32[]{:S(2)}, u32[]{:S(2)}) collective-permute-start(f32[2,4,16,256]{3,2,1,0:T(8,128)S(1)} %get-tuple-element.133.last), channel_id=1, source_target_pairs={{0,30},{8,6},{16,14},{24,22},{2,0},{10,8},{18,16},{26,24},{4,2},{1... | collective-permute-start | bytes 393224 | tf_op jit(solution)/shard_map/ppermute | solution.py:39
  128.3 7.4 %collective-permute-start.14 = (f32[2,4,16,256]{3,2,1,0:T(8,128)S(1)}, f32[2,4,16,256]{3,2,1,0:T(8,128)S(1)}, u32[]{:S(2)}, u32[]{:S(2)}) collective-permute-start(f32[2,4,16,256]{3,2,1,0:T(8,128)S(1)} %param.20), channel_id=1, source_target_pairs={{0,4},{8,12},{16,20},{24,28},{2,6},{10,14},{18,22},{26,30},{4,8},{... | collective-permute-start | bytes 393224 | tf_op jit(solution)/shard_map/cond/branch_4_fun/ppermute | solution.py:39
  136.4 4.1 %collective-permute-start.42 = (f32[4,16,256]{2,1,0:T(8,128)S(1)}, f32[4,16,256]{2,1,0:T(8,128)S(1)}, u32[]{:S(2)}, u32[]{:S(2)}) collective-permute-start(f32[4,16,256]{2,1,0:T(8,128)S(1)} %get-tuple-element.136), channel_id=1, source_target_pairs={{0,32},{8,40},{16,48},{24,56},{2,34},{10,42},{18,50},{26,58},{4,36... | collective-permute-start | bytes 196616 | tf_op jit(solution)/shard_map/ppermute | solution.py:39

commit v2 on v1

--- a/solution.py
+++ b/solution.py
@@ -196,30 +196,31 @@
         def _(b=b, out=out, k=k):
             pltpu.make_async_copy(b, out, sems.at[k]).start()
 
-    for k, (a, _, out) in enumerate(choices):
-        pltpu.make_async_copy(a, out, sems.at[k]).wait()
+    return [pltpu.make_async_copy(a, out, sems.at[k]) for k, (a, _, out) in enumerate(choices)]
 
 
 def plan_kernel(ids, offsets, velocity, epsilon, delta, angle, plan, turn_z, turn_y, own, other, sems):
+    copies = fetch(
+        ids[0] & 1 == 0,
+        (
+            (delta, velocity, other.at[0]),
+            (angle, epsilon, other.at[1]),
+            (velocity, delta, own.at[0]),
+            (epsilon, angle, own.at[1]),
+        ),
+        sems,
+    )
     values, free_turn = plan_values(ids, [offsets[g] for g in range(4)])
     for k, v in values.items():
         plan[k] = v
     turn_z[0] = free_turn >> 3
     turn_y[0] = free_turn & 7
-    fetch(
-        values[CORE] == 0,
-        (
-            (velocity, delta, own.at[0]),
-            (epsilon, angle, own.at[1]),
-            (delta, velocity, other.at[0]),
-            (angle, epsilon, other.at[1]),
-        ),
-        sems,
-    )
+    for copy in copies:
+        copy.wait()
 
 
 def state_kernel(plan, fwd_now, adj_now, fwd_before, adj_before, one, two, sems):
-    fetch(
+    copies = fetch(
         plan[X_HI] == 0,
         (
             (adj_now.at[0], fwd_now.at[0], one.at[0]),
@@ -229,6 +230,8 @@
         ),
         sems,
     )
+    for copy in copies:
+        copy.wait()
 
 
 def rows_kernel(plan, own, came, last, free):
@@ -263,7 +266,8 @@
                 outs[by][f, i] = jnp.where(role[by] == 0, straight, turned)
 
 
-def tiles_kernel(plan, kept, got_1, got_2, got_3, out):
+def tiles_kernel(plan, kept, got_1, got_2, got_3, low, high, out):
+    del low, high
     source = [plan[SOURCE + h] for h in range(2)]
     for f in range(2):
         for i in range(TX):
@@ -442,7 +446,11 @@
 
 
 HBM = pl.BlockSpec(memory_space=pltpu.HBM)
-LIMIT = pltpu.CompilerParams(vmem_limit_bytes=8 * 1024 * 1024)
+LIMIT = pltpu.CompilerParams(vmem_limit_bytes=4 * 1024 * 1024)
+
+
+def in_hbm(value):
+    return pltpu.with_memory_space_constraint(value, pltpu.HBM)
 
 
 def call(kernel, n_in, outs, scratch=()):
@@ -501,7 +509,7 @@
         out_specs=[SMEM] * 3 + [VMEM] * 2,
         scratch_shapes=[pltpu.SemaphoreType.DMA((4,))],
         compiler_params=LIMIT,
-    )(ids, offsets, velocity, thomsen_epsilon, thomsen_delta, tilt_angle)
+    )(ids, offsets, *(in_hbm(v) for v in (velocity, thomsen_epsilon, thomsen_delta, tilt_angle)))
     came = send(other, swap)
     one, two = pl.pallas_call(
         state_kernel,
@@ -510,7 +518,7 @@
         out_specs=[VMEM] * 2,
         scratch_shapes=[pltpu.SemaphoreType.DMA((4,))],
         compiler_params=LIMIT,
-    )(plan, fwd_now, adj_now, fwd_before, adj_before)
+    )(plan, *(in_hbm(v) for v in (fwd_now, adj_now, fwd_before, adj_before)))
     got_one, got_two = send(one, state_first()), send(two, state_second())
 
     last, free = call(rows_kernel, 2, [TILE] * 2)(plan, own, came)
@@ -520,7 +528,8 @@
         plan, own, came, last, last_came, free_came, two, got_one, got_two
     )
     got = [send(rows[by], across(by)) for by in range(1, 4)]
-    tiles = call(tiles_kernel, 4, [(2,) + TILE])(plan, rows[0], *got)[0]
+    low, high = send(hi, up), send(lo, down)
+    tiles = call(tiles_kernel, 6, [(2,) + TILE])(plan, rows[0], *got, low, high)[0]
     coef = call(coef_kernel, 2, [(6, 8, AY, AZ)])(plan, tiles, send(tiles, swap))[0]
 
     n_rec = receiver_cell.shape[1]
@@ -536,7 +545,8 @@
 
     shared = None
     for k in range(STEPS - 1):
-        low, high = send(hi, up), send(lo, down)
+        if k > 0:
+            low, high = send(hi, up), send(lo, down)
         outs = [TILE, TILE] + ([(2, 2, TX, AY, AZ)] if k == 1 else [])
         new = call(step_kernel, 8, outs, [(2, 4 * TX, AY, AZ)])(
             plan, lo, hi, lo_b, hi_b, low, high, coef, inj[k]

time: 141 us -> 126 us (0.89); the launches traced: 142 us -> 124 us
  local copies, waits for them, and re-layouts: 12.6 us -> 4.5 us
  starting transfers between devices: 56 us -> 48.8 us
  waiting for transfers between devices: 45 us -> 41.2 us
    unnamed x30 -> x14, local copies, waits for them, and re-layouts: 11.1 us -> 3.04 us
    ppermute x25 -> x23, starting transfers between devices: 56 us -> 48.8 us  [send(): return lax.ppermute(value, AXES, pairs)]
    ppermute x25 -> x23, waiting for transfers between devices: 45 us -> 41.2 us  [send(): return lax.ppermute(value, AXES, pairs)]
  transfers between devices with their start and end apart: 25 -> 23, of which waited for: 14 -> 11; matrix products, arithmetic and copies ran while one was open for 2% -> 2% of each run, Pallas kernels for 5% -> 6%
where the time goes in v2:
time: 126 us; the launch traced here: 124 us
  starting transfers between devices  48.8 us (39%)
  waiting for transfers between devices  41.2 us (33%)
  Pallas kernels  26.9 us (21%)
  local copies, waits for them, and re-layouts  4.5 us (4%)
  between operations  1.52 us (1%)
    ppermute x23, starting transfers between devices, send(): return lax.ppermute(value, AXES, pairs)  48.8 us
    ppermute x23, waiting for transfers between devices, send(): return lax.ppermute(value, AXES, pairs)  41.2 us
    pallas_call x3, Pallas kernels, local(): call(step_kernel, 8, outs, [(2, 4 * TX, AY, AZ)])  10.5 us
    pallas_call x1, Pallas kernels, local(): call(last_kernel, 9, [(2,) + PART] * 2, [(2, 4 * TX, AY, AZ), (2, TX, AY,...  3.52 us
    unnamed x14, local copies, waits for them, and re-layouts  3.04 us
  transfers between devices with their start and end apart: 23, of which 11 were waited for; matrix products, arithmetic and copies ran while one was open for 2% of the time, Pallas kernels for 6%

profile of v2, /device:TPU:1, one launch (start us, length us, event | category | flops | bytes accessed | tf_op | source)
XLA Modules:
  0.0 123.9 jit_solution(9248296365218226644)
XLA Ops:
  0.0 0.1 pad_add_fusion.ids
  0.1 0.7 copy-done.5
  0.7 2.3 %shard_map.127 = (s32[40]{0:T(128)S(1)}, s32[1]{0:T(128)}, s32[1]{0:T(128)}, f32[2,4,32,256]{3,2,1,0:T(8,128)S(1)}, f32[2,4,32,256]{3,2,1,0:T(8,128)S(1)}) custom-call(s32[2]{0:T(128)S(1)} %pad_add_fusion.ids, s32[4]{0:T(128)S(1)} %copy-done.5, f32[4,32,256]{2,1,0:T(8,128)} %velocity.1, f32[4,32,256]{2,1,0:T(8,128)} %epsilon.1, f32[4,32,256]{2,1,0:T(8,128)} %delta.1, ...), custom_call_target="tpu_custom_call" | custom-call | tf_op jit(solution)/shard_map/pallas_call | solution.py:505
  3.0 1.5 %collective-permute-start.20 = (f32[2,4,32,256]{3,2,1,0:T(8,128)S(1)}, f32[2,4,32,256]{3,2,1,0:T(8,128)S(1)}, u32[]{:S(2)}, u32[]{:S(2)}) collective-permute-start(f32[2,4,32,256]{3,2,1,0:T(8,128)S(1)} %get-tuple-element.104), channel_id=1, source_target_pairs={{0,32},{8,40},{16,48},{24,56},{2,34},{10,42},{18,50},{26,58},{4,36... | collective-permute-start | bytes 786440 | tf_op jit(solution)/shard_map/ppermute | solution.py:39
  4.5 1.8 %shard_map.129 = (f32[2,2,4,32,256]{4,3,2,1,0:T(8,128)S(1)}, f32[2,2,4,32,256]{4,3,2,1,0:T(8,128)S(1)}) custom-call(s32[40]{0:T(128)S(1)} %get-tuple-element.102.plan, f32[1,2,4,32,256]{4,3,2,1,0:T(8,128)} %fwd_now.1, f32[1,2,4,32,256]{4,3,2,1,0:T(8,128)} %adj_now.1, f32[1,2,4,32,256]{4,3,2,1,0:T(8,128)} %fwd_before.1, f32[1,2,4,32,256]{4,3,2,1,0:T(8,128)} %adj_before.1), custom_call_target="tpu_custom_call" | custom-call | tf_op jit(solution)/shard_map/pallas_call | solution.py:514
  6.3 4.6 %collective-permute-start.23 = (f32[2,2,4,32,256]{4,3,2,1,0:T(8,128)S(1)}, f32[2,2,4,32,256]{4,3,2,1,0:T(8,128)S(1)}, u32[]{:S(2)}, u32[]{:S(2)}) collective-permute-start(f32[2,2,4,32,256]{4,3,2,1,0:T(8,128)S(1)} %get-tuple-element.109.kept), channel_id=1, source_target_pairs={{32,1},{40,9},{48,17},{56,25},{34,3},{42,11},{50,19},{58,27},{36,5... | collective-permute-start | bytes 1572872 | tf_op jit(solution)/shard_map/ppermute | solution.py:39
  10.9 0.1 collective-permute-start.22
  11.0 0.0 collective-permute-done.20.came
  11.0 0.6 shard_map.128
  11.6 1.4 %collective-permute-start.21 = (f32[2,4,32,256]{3,2,1,0:T(8,128)S(1)}, f32[2,4,32,256]{3,2,1,0:T(8,128)S(1)}, u32[]{:S(2)}, u32[]{:S(2)}) collective-permute-start(f32[2,4,32,256]{3,2,1,0:T(8,128)S(1)} %get-tuple-element.105.last), channel_id=1, source_target_pairs={{0,2},{8,10},{16,18},{24,26},{2,4},{10,12},{18,20},{26,28},{4,6},{... | collective-permute-start | bytes 786440 | tf_op jit(solution)/shard_map/ppermute | solution.py:39
  14.4 9.8 %collective-permute-done.21.last_came = f32[2,4,32,256]{3,2,1,0:T(8,128)S(1)} collective-permute-done((f32[2,4,32,256]{3,2,1,0:T(8,128)S(1)}, f32[2,4,32,256]{3,2,1,0:T(8,128)S(1)}, u32[]{:S(2)}, u32[]{:S(2)}) %collective-permute-start.21) | collective-permute-done | bytes 262176 | tf_op jit(solution)/shard_map/ppermute | solution.py:39
  24.2 0.0 collective-permute-done.22.one
  24.2 2.0 %shard_map.130 = (f32[2,4,32,256]{3,2,1,0:T(8,128)S(1)}, f32[2,4,32,256]{3,2,1,0:T(8,128)}, f32[2,4,32,256]{3,2,1,0:T(8,128)}, f32[2,4,32,256]{3,2,1,0:T(8,128)}...) custom-call(s32[40]{0:T(128)S(1)} %get-tuple-element.102.plan, ...), custom_call_target="tpu_custom_call" | custom-call | tf_op jit(solution)/shard_map/pallas_call | solution.py:527
  26.1 0.7 copy-done.1
  26.8 0.7 copy-done.3
  27.5 4.8 %collective-permute-start.25 = (f32[2,4,32,256]{3,2,1,0:T(8,128)S(1)}, f32[2,4,32,256]{3,2,1,0:T(8,128)S(1)}, u32[]{:S(2)}, u32[]{:S(2)}) collective-permute-start(f32[2,4,32,256]{3,2,1,0:T(8,128)S(1)} %get-tuple-element.111.lo.lo_b), channel_id=1, source_target_pairs={{0,30},{8,6},{16,14},{24,22},{2,0},{10,8},{18,16},{26,24},{4,2},{1... | collective-permute-start | bytes 786440 | tf_op jit(solution)/shard_map/ppermute | solution.py:39
  32.3 0.3 collective-permute-start.26
  32.6 3.9 %collective-permute-start.27 = (f32[2,4,32,256]{3,2,1,0:T(8,128)}, f32[2,4,32,256]{3,2,1,0:T(8,128)S(1)}, u32[]{:S(2)}, u32[]{:S(2)}) collective-permute-start(f32[2,4,32,256]{3,2,1,0:T(8,128)} %get-tuple-element.117), channel_id=1, source_target_pairs={{0,1},{8,9},{16,17},{24,25},{2,3},{10,11},{18,19},{26,27},{4,5},{1... | collective-permute-start | bytes 786440 | tf_op jit(solution)/shard_map/ppermute | solution.py:39
  36.6 1.2 collective-permute-start.28
  37.7 0.7 fusion.1
  38.4 0.8 bitcast_select_fusion.1.amounts
  39.2 0.0 collective-permute-done.24.low
  39.2 0.0 collective-permute-done.25.high
  39.2 0.9 collective-permute-done.26.got_1
  40.1 8.8 %collective-permute-done.27.got_2 = f32[2,4,32,256]{3,2,1,0:T(8,128)S(1)} collective-permute-done((f32[2,4,32,256]{3,2,1,0:T(8,128)}, f32[2,4,32,256]{3,2,1,0:T(8,128)S(1)}, u32[]{:S(2)}, u32[]{:S(2)}) %collective-permute-start.27) | collective-permute-done | bytes 262176 | tf_op jit(solution)/shard_map/ppermute | solution.py:39
  48.9 0.9 copy-done.4
  49.9 0.6 shard_map.131.own
  50.5 0.8 collective-permute-start.29
  51.3 0.7 fusion
  52.0 0.1 bitcast_select_fusion.cells
  52.1 1.6 %shard_map.133 = f32[4,8,32,256]{3,2,1,0:T(8,128)S(1)} custom-call(s32[40]{0:T(128)S(1)} %get-tuple-element.102.plan, s32[3,256]{1,0:T(4,128)S(1)} %bitcast_select_fusion.cells, f32[4,256]{1,0:T(4,128)S(1)} %bitcast_select_fusion.1.amounts), custom_call_target="tpu_custom_call" | custom-call | tf_op jit(solution)/shard_map/pallas_call | solution.py:544
  53.7 0.1 slice_bitcast_fusion
  53.8 1.0 shard_map.132.coef
  54.8 3.5 %shard_map.134 = (f32[2,4,32,256]{3,2,1,0:T(8,128)S(1)}, f32[2,4,32,256]{3,2,1,0:T(8,128)S(1)}) custom-call(s32[40]{0:T(128)S(1)} %get-tuple-element.102.plan, f32[2,4,32,256]{3,2,1,0:T(8,128)S(1)} %get-tuple-element.111.lo.lo_b, f32[2,4,32,256]{3,2,1,0:T(8,128)S(1)} %get-tuple-element.112.hi.hi_b, f32[2,4,32,256]{3,2,1,0:T(8,128)S(1)} %get-tuple-element.113.lo_b, ...), custom_call_target="tpu_custom_call" | custom-call | tf_op jit(solution)/shard_map/pallas_call | solution.py:551
  58.4 0.1 collective-permute-start.30
  58.4 4.8 %collective-permute-start.31 = (f32[2,4,32,256]{3,2,1,0:T(8,128)S(1)}, f32[2,4,32,256]{3,2,1,0:T(8,128)S(1)}, u32[]{:S(2)}, u32[]{:S(2)}) collective-permute-start(f32[2,4,32,256]{3,2,1,0:T(8,128)S(1)} %get-tuple-element.119.lo.lo_b), channel_id=1, source_target_pairs={{0,30},{8,6},{16,14},{24,22},{2,0},{10,8},{18,16},{26,24},{4,2},{1... | collective-permute-start | bytes 786440 | tf_op jit(solution)/shard_map/ppermute | solution.py:39
  63.2 6.5 %collective-permute-done.30.low = f32[2,4,32,256]{3,2,1,0:T(8,128)S(1)} collective-permute-done((f32[2,4,32,256]{3,2,1,0:T(8,128)S(1)}, f32[2,4,32,256]{3,2,1,0:T(8,128)S(1)}, u32[]{:S(2)}, u32[]{:S(2)}) %collective-permute-start.30) | collective-permute-done | bytes 262176 | tf_op jit(solution)/shard_map/ppermute | solution.py:39
  69.7 3.5 %shard_map.135 = (f32[2,4,32,256]{3,2,1,0:T(8,128)S(1)}, f32[2,4,32,256]{3,2,1,0:T(8,128)S(1)}, f32[2,2,4,32,256]{4,3,2,1,0:T(8,128)S(1)}) custom-call(s32[40]{0:T(128)S(1)} %get-tuple-element.102.plan, f32[2,4,32,256]{3,2,1,0:T(8,128)S(1)} %get-tuple-element.119.lo.lo_b, f32[2,4,32,256]{3,2,1,0:T(8,128)S(1)} %get-tuple-element.120.hi.hi_b, ...), custom_call_target="tpu_custom_call" | custom-call | tf_op jit(solution)/shard_map/pallas_call | solution.py:551
  73.2 0.3 collective-permute-start.32
  73.4 4.8 %collective-permute-start.33 = (f32[2,4,32,256]{3,2,1,0:T(8,128)S(1)}, f32[2,4,32,256]{3,2,1,0:T(8,128)S(1)}, u32[]{:S(2)}, u32[]{:S(2)}) collective-permute-start(f32[2,4,32,256]{3,2,1,0:T(8,128)S(1)} %get-tuple-element.121.lo.lo_b), channel_id=1, source_target_pairs={{0,30},{8,6},{16,14},{24,22},{2,0},{10,8},{18,16},{26,24},{4,2},{1... | collective-permute-start | bytes 786440 | tf_op jit(solution)/shard_map/ppermute | solution.py:39
  78.2 1.4 %collective-permute-start.36 = (f32[2,2,4,32,256]{4,3,2,1,0:T(8,128)S(1)}, f32[2,2,4,32,256]{4,3,2,1,0:T(8,128)S(1)}, u32[]{:S(2)}, u32[]{:S(2)}) collective-permute-start(f32[2,2,4,32,256]{4,3,2,1,0:T(8,128)S(1)} %get-tuple-element.125), channel_id=1, source_target_pairs={{0,32},{8,40},{16,48},{24,56},{2,34},{10,42},{18,50},{26,58},{4,36... | collective-permute-start | bytes 1572872 | tf_op jit(solution)/shard_map/ppermute | solution.py:39
  79.6 4.2 %collective-permute-done.32.low = f32[2,4,32,256]{3,2,1,0:T(8,128)S(1)} collective-permute-done((f32[2,4,32,256]{3,2,1,0:T(8,128)S(1)}, f32[2,4,32,256]{3,2,1,0:T(8,128)S(1)}, u32[]{:S(2)}, u32[]{:S(2)}) %collective-permute-start.32) | collective-permute-done | bytes 262176 | tf_op jit(solution)/shard_map/ppermute | solution.py:39
  83.8 0.0 collective-permute-done.33.high
  83.8 3.5 %shard_map.136 = (f32[2,4,32,256]{3,2,1,0:T(8,128)S(1)}, f32[2,4,32,256]{3,2,1,0:T(8,128)S(1)}) custom-call(s32[40]{0:T(128)S(1)} %get-tuple-element.102.plan, f32[2,4,32,256]{3,2,1,0:T(8,128)S(1)} %get-tuple-element.121.lo.lo_b, f32[2,4,32,256]{3,2,1,0:T(8,128)S(1)} %get-tuple-element.122.hi.hi_b, f32[2,4,32,256]{3,2,1,0:T(8,128)S(1)} %get-tuple-element.119.lo.lo_b, ...), custom_call_target="tpu_custom_call" | custom-call | tf_op jit(solution)/shard_map/pallas_call | solution.py:551
  87.3 0.1 collective-permute-start.34
  87.4 4.8 %collective-permute-start.35 = (f32[2,4,32,256]{3,2,1,0:T(8,128)S(1)}, f32[2,4,32,256]{3,2,1,0:T(8,128)S(1)}, u32[]{:S(2)}, u32[]{:S(2)}) collective-permute-start(f32[2,4,32,256]{3,2,1,0:T(8,128)S(1)} %get-tuple-element.123.lo), channel_id=1, source_target_pairs={{0,30},{8,6},{16,14},{24,22},{2,0},{10,8},{18,16},{26,24},{4,2},{1... | collective-permute-start | bytes 786440 | tf_op jit(solution)/shard_map/ppermute | solution.py:39
  92.2 4.6 %collective-permute-done.34.low = f32[2,4,32,256]{3,2,1,0:T(8,128)S(1)} collective-permute-done((f32[2,4,32,256]{3,2,1,0:T(8,128)S(1)}, f32[2,4,32,256]{3,2,1,0:T(8,128)S(1)}, u32[]{:S(2)}, u32[]{:S(2)}) %collective-permute-start.34) | collective-permute-done | bytes 262176 | tf_op jit(solution)/shard_map/ppermute | solution.py:39
  96.8 0.0 collective-permute-done.35.high
  96.8 3.5 %shard_map.137 = (f32[2,4,16,256]{3,2,1,0:T(8,128)S(1)}, f32[2,4,16,256]{3,2,1,0:T(8,128)S(1)}) custom-call(s32[40]{0:T(128)S(1)} %get-tuple-element.102.plan, f32[2,4,32,256]{3,2,1,0:T(8,128)S(1)} %get-tuple-element.123.lo, f32[2,4,32,256]{3,2,1,0:T(8,128)S(1)} %get-tuple-element.124.hi, f32[2,4,32,256]{3,2,1,0:T(8,128)S(1)} %get-tuple-element.121.lo.lo_b, ...), custom_call_target="tpu_custom_call" | custom-call | tf_op jit(solution)/shard_map/pallas_call | solution.py:558
  100.3 2.7 %collective-permute-start.37 = (f32[2,4,16,256]{3,2,1,0:T(8,128)S(1)}, f32[2,4,16,256]{3,2,1,0:T(8,128)S(1)}, u32[]{:S(2)}, u32[]{:S(2)}) collective-permute-start(f32[2,4,16,256]{3,2,1,0:T(8,128)S(1)} %get-tuple-element.127), channel_id=1, source_target_pairs={{0,32},{8,40},{16,48},{24,56},{2,34},{10,42},{18,50},{26,58},{4,36... | collective-permute-start | bytes 393224 | tf_op jit(solution)/shard_map/ppermute | solution.py:39
  103.0 1.0 collective-permute-done.37.came
  104.0 0.6 shard_map.138
  104.6 0.9 collective-permute-start.38
  105.5 2.1 %collective-permute-start.39 = (f32[4,16,256]{2,1,0:T(8,128)S(1)}, f32[4,16,256]{2,1,0:T(8,128)S(1)}, u32[]{:S(2)}, u32[]{:S(2)}) collective-permute-start(f32[4,16,256]{2,1,0:T(8,128)S(1)} %get-tuple-element.130), channel_id=1, source_target_pairs={{0,1},{8,9},{16,17},{24,25},{2,3},{10,11},{18,19},{26,27},{4,5},{1... | collective-permute-start | bytes 196616 | tf_op jit(solution)/shard_map/ppermute | solution.py:39
  107.6 1.5 %collective-permute-start.40 = (f32[4,16,256]{2,1,0:T(8,128)S(1)}, f32[4,16,256]{2,1,0:T(8,128)S(1)}, u32[]{:S(2)}, u32[]{:S(2)}) collective-permute-start(f32[4,16,256]{2,1,0:T(8,128)S(1)} %get-tuple-element.131), channel_id=1, source_target_pairs={{0,65},{8,73},{16,81},{24,89},{2,67},{10,75},{18,83},{26,91},{4,69... | collective-permute-start | bytes 196616 | tf_op jit(solution)/shard_map/ppermute | solution.py:39
  109.1 2.0 %collective-permute-done.39.got_2 = f32[4,16,256]{2,1,0:T(8,128)S(1)} collective-permute-done((f32[4,16,256]{2,1,0:T(8,128)S(1)}, f32[4,16,256]{2,1,0:T(8,128)S(1)}, u32[]{:S(2)}, u32[]{:S(2)}) %collective-permute-start.39) | collective-permute-done | bytes 65568 | tf_op jit(solution)/shard_map/ppermute | solution.py:39
  111.1 0.5 collective-permute-done.40.got_3
  111.7 0.7 shard_map.139
  112.3 4.8 %collective-permute-start.41 = (f32[2,4,16,256]{3,2,1,0:T(8,128)S(1)}, f32[2,4,16,256]{3,2,1,0:T(8,128)S(1)}, u32[]{:S(2)}, u32[]{:S(2)}) collective-permute-start(f32[2,4,16,256]{3,2,1,0:T(8,128)S(1)} %get-tuple-element.133.last), channel_id=1, source_target_pairs={{0,30},{8,6},{16,14},{24,22},{2,0},{10,8},{18,16},{26,24},{4,2},{1... | collective-permute-start | bytes 393224 | tf_op jit(solution)/shard_map/ppermute | solution.py:39
  117.2 1.9 %collective-permute-done.41.last_came = f32[2,4,16,256]{3,2,1,0:T(8,128)S(1)} collective-permute-done((f32[2,4,16,256]{3,2,1,0:T(8,128)S(1)}, f32[2,4,16,256]{3,2,1,0:T(8,128)S(1)}, u32[]{:S(2)}, u32[]{:S(2)}) %collective-permute-start.41) | collective-permute-done | bytes 131104 | tf_op jit(solution)/shard_map/ppermute | solution.py:39
  119.1 0.6 shard_map.140
  119.7 2.1 %collective-permute-start.42 = (f32[4,16,256]{2,1,0:T(8,128)S(1)}, f32[4,16,256]{2,1,0:T(8,128)S(1)}, u32[]{:S(2)}, u32[]{:S(2)}) collective-permute-start(f32[4,16,256]{2,1,0:T(8,128)S(1)} %get-tuple-element.136), channel_id=1, source_target_pairs={{0,32},{8,40},{16,48},{24,56},{2,34},{10,42},{18,50},{26,58},{4,36... | collective-permute-start | bytes 196616 | tf_op jit(solution)/shard_map/ppermute | solution.py:39
  121.8 0.9 collective-permute-done.42.came
  122.7 1.2 shard_map.141
  (23 shorter events, 0.1 us)
Async XLA Ops:
  0.0 14.3 %copy-start = (s32[4,256,3]{1,0,2:T(4,128)S(1)}, s32[4,256,3]{1,0,2:T(4,128)}, u32[]{:S(2)}) copy-start(s32[4,256,3]{1,0,2:T(4,128)} %param.49) | copy-start | bytes 36868
  0.1 0.7 copy-start.5
  3.0 8.0 %collective-permute-start.20 = (f32[2,4,32,256]{3,2,1,0:T(8,128)S(1)}, f32[2,4,32,256]{3,2,1,0:T(8,128)S(1)}, u32[]{:S(2)}, u32[]{:S(2)}) collective-permute-start(f32[2,4,32,256]{3,2,1,0:T(8,128)S(1)} %get-tuple-element.104), channel_id=1, source_target_pairs={{0,32},{8,40},{16,48},{24,56},{2,34},{10,42},{18,50},{26,58},{4,36... | collective-permute-start | bytes 786440 | tf_op jit(solution)/shard_map/ppermute | solution.py:39
  6.3 17.9 %collective-permute-start.23 = (f32[2,2,4,32,256]{4,3,2,1,0:T(8,128)S(1)}, f32[2,2,4,32,256]{4,3,2,1,0:T(8,128)S(1)}, u32[]{:S(2)}, u32[]{:S(2)}) collective-permute-start(f32[2,2,4,32,256]{4,3,2,1,0:T(8,128)S(1)} %get-tuple-element.109.kept), channel_id=1, source_target_pairs={{32,1},{40,9},{48,17},{56,25},{34,3},{42,11},{50,19},{58,27},{36,5... | collective-permute-start | bytes 1572872 | tf_op jit(solution)/shard_map/ppermute | solution.py:39
  10.9 13.2 %collective-permute-start.22 = (f32[2,2,4,32,256]{4,3,2,1,0:T(8,128)S(1)}, f32[2,2,4,32,256]{4,3,2,1,0:T(8,128)S(1)}, u32[]{:S(2)}, u32[]{:S(2)}) collective-permute-start(f32[2,2,4,32,256]{4,3,2,1,0:T(8,128)S(1)} %get-tuple-element.110), channel_id=1, source_target_pairs={{0,32},{8,40},{16,48},{24,56},{2,34},{10,42},{18,50},{26,58},{4,36... | collective-permute-start | bytes 1572872 | tf_op jit(solution)/shard_map/ppermute | solution.py:39
  11.6 12.5 %collective-permute-start.21 = (f32[2,4,32,256]{3,2,1,0:T(8,128)S(1)}, f32[2,4,32,256]{3,2,1,0:T(8,128)S(1)}, u32[]{:S(2)}, u32[]{:S(2)}) collective-permute-start(f32[2,4,32,256]{3,2,1,0:T(8,128)S(1)} %get-tuple-element.105.last), channel_id=1, source_target_pairs={{0,2},{8,10},{16,18},{24,26},{2,4},{10,12},{18,20},{26,28},{4,6},{... | collective-permute-start | bytes 786440 | tf_op jit(solution)/shard_map/ppermute | solution.py:39
  14.4 9.8 %copy-start.6 = (f32[2,4,32,256]{3,2,1,0:T(8,128)}, f32[2,4,32,256]{3,2,1,0:T(8,128)S(1)}, u32[]{:S(2)}) copy-start(f32[2,4,32,256]{3,2,1,0:T(8,128)S(1)} %get-tuple-element.142.free_came) | copy-start | bytes 786436
  26.1 0.7 copy-start.1
  26.8 0.7 copy-start.3
  27.5 11.6 %collective-permute-start.24 = (f32[2,4,32,256]{3,2,1,0:T(8,128)S(1)}, f32[2,4,32,256]{3,2,1,0:T(8,128)S(1)}, u32[]{:S(2)}, u32[]{:S(2)}) collective-permute-start(f32[2,4,32,256]{3,2,1,0:T(8,128)S(1)} %get-tuple-element.112.hi.hi_b), channel_id=1, source_target_pairs={{0,2},{8,10},{16,18},{24,26},{2,4},{10,12},{18,20},{26,28},{4,6},{... | collective-permute-start | bytes 786440 | tf_op jit(solution)/shard_map/ppermute | solution.py:39
  27.5 11.6 %collective-permute-start.25 = (f32[2,4,32,256]{3,2,1,0:T(8,128)S(1)}, f32[2,4,32,256]{3,2,1,0:T(8,128)S(1)}, u32[]{:S(2)}, u32[]{:S(2)}) collective-permute-start(f32[2,4,32,256]{3,2,1,0:T(8,128)S(1)} %get-tuple-element.111.lo.lo_b), channel_id=1, source_target_pairs={{0,30},{8,6},{16,14},{24,22},{2,0},{10,8},{18,16},{26,24},{4,2},{1... | collective-permute-start | bytes 786440 | tf_op jit(solution)/shard_map/ppermute | solution.py:39
  32.3 7.8 %collective-permute-start.26 = (f32[2,4,32,256]{3,2,1,0:T(8,128)}, f32[2,4,32,256]{3,2,1,0:T(8,128)S(1)}, u32[]{:S(2)}, u32[]{:S(2)}) collective-permute-start(f32[2,4,32,256]{3,2,1,0:T(8,128)} %get-tuple-element.116), channel_id=1, source_target_pairs={{0,64},{8,72},{16,80},{24,88},{2,66},{10,74},{18,82},{26,90},{4,68... | collective-permute-start | bytes 786440 | tf_op jit(solution)/shard_map/ppermute | solution.py:39
  32.6 16.3 %collective-permute-start.27 = (f32[2,4,32,256]{3,2,1,0:T(8,128)}, f32[2,4,32,256]{3,2,1,0:T(8,128)S(1)}, u32[]{:S(2)}, u32[]{:S(2)}) collective-permute-start(f32[2,4,32,256]{3,2,1,0:T(8,128)} %get-tuple-element.117), channel_id=1, source_target_pairs={{0,1},{8,9},{16,17},{24,25},{2,3},{10,11},{18,19},{26,27},{4,5},{1... | collective-permute-start | bytes 786440 | tf_op jit(solution)/shard_map/ppermute | solution.py:39
  36.6 12.4 %collective-permute-start.28 = (f32[2,4,32,256]{3,2,1,0:T(8,128)}, f32[2,4,32,256]{3,2,1,0:T(8,128)S(1)}, u32[]{:S(2)}, u32[]{:S(2)}) collective-permute-start(f32[2,4,32,256]{3,2,1,0:T(8,128)} %get-tuple-element.118), channel_id=1, source_target_pairs={{0,65},{8,73},{16,81},{24,89},{2,67},{10,75},{18,83},{26,91},{4,69... | collective-permute-start | bytes 786440 | tf_op jit(solution)/shard_map/ppermute | solution.py:39
  48.9 1.0 copy-start.4
  50.5 3.3 %collective-permute-start.29 = (f32[2,2,4,32,256]{4,3,2,1,0:T(8,128)S(1)}, f32[2,2,4,32,256]{4,3,2,1,0:T(8,128)S(1)}, u32[]{:S(2)}, u32[]{:S(2)}) collective-permute-start(f32[2,2,4,32,256]{4,3,2,1,0:T(8,128)S(1)} %shard_map.131.own), channel_id=1, source_target_pairs={{0,32},{8,40},{16,48},{24,56},{2,34},{10,42},{18,50},{26,58},{4,36... | collective-permute-start | bytes 1572872 | tf_op jit(solution)/shard_map/ppermute | solution.py:39
  53.8 1.0 copy-start.2
  58.4 11.3 %collective-permute-start.30 = (f32[2,4,32,256]{3,2,1,0:T(8,128)S(1)}, f32[2,4,32,256]{3,2,1,0:T(8,128)S(1)}, u32[]{:S(2)}, u32[]{:S(2)}) collective-permute-start(f32[2,4,32,256]{3,2,1,0:T(8,128)S(1)} %get-tuple-element.120.hi.hi_b), channel_id=1, source_target_pairs={{0,2},{8,10},{16,18},{24,26},{2,4},{10,12},{18,20},{26,28},{4,6},{... | collective-permute-start | bytes 786440 | tf_op jit(solution)/shard_map/ppermute | solution.py:39
  58.4 11.2 %collective-permute-start.31 = (f32[2,4,32,256]{3,2,1,0:T(8,128)S(1)}, f32[2,4,32,256]{3,2,1,0:T(8,128)S(1)}, u32[]{:S(2)}, u32[]{:S(2)}) collective-permute-start(f32[2,4,32,256]{3,2,1,0:T(8,128)S(1)} %get-tuple-element.119.lo.lo_b), channel_id=1, source_target_pairs={{0,30},{8,6},{16,14},{24,22},{2,0},{10,8},{18,16},{26,24},{4,2},{1... | collective-permute-start | bytes 786440 | tf_op jit(solution)/shard_map/ppermute | solution.py:39
  73.2 10.6 %collective-permute-start.32 = (f32[2,4,32,256]{3,2,1,0:T(8,128)S(1)}, f32[2,4,32,256]{3,2,1,0:T(8,128)S(1)}, u32[]{:S(2)}, u32[]{:S(2)}) collective-permute-start(f32[2,4,32,256]{3,2,1,0:T(8,128)S(1)} %get-tuple-element.122.hi.hi_b), channel_id=1, source_target_pairs={{0,2},{8,10},{16,18},{24,26},{2,4},{10,12},{18,20},{26,28},{4,6},{... | collective-permute-start | bytes 786440 | tf_op jit(solution)/shard_map/ppermute | solution.py:39
  73.4 10.3 %collective-permute-start.33 = (f32[2,4,32,256]{3,2,1,0:T(8,128)S(1)}, f32[2,4,32,256]{3,2,1,0:T(8,128)S(1)}, u32[]{:S(2)}, u32[]{:S(2)}) collective-permute-start(f32[2,4,32,256]{3,2,1,0:T(8,128)S(1)} %get-tuple-element.121.lo.lo_b), channel_id=1, source_target_pairs={{0,30},{8,6},{16,14},{24,22},{2,0},{10,8},{18,16},{26,24},{4,2},{1... | collective-permute-start | bytes 786440 | tf_op jit(solution)/shard_map/ppermute | solution.py:39
  78.2 18.6 %collective-permute-start.36 = (f32[2,2,4,32,256]{4,3,2,1,0:T(8,128)S(1)}, f32[2,2,4,32,256]{4,3,2,1,0:T(8,128)S(1)}, u32[]{:S(2)}, u32[]{:S(2)}) collective-permute-start(f32[2,2,4,32,256]{4,3,2,1,0:T(8,128)S(1)} %get-tuple-element.125), channel_id=1, source_target_pairs={{0,32},{8,40},{16,48},{24,56},{2,34},{10,42},{18,50},{26,58},{4,36... | collective-permute-start | bytes 1572872 | tf_op jit(solution)/shard_map/ppermute | solution.py:39
  87.3 9.5 %collective-permute-start.34 = (f32[2,4,32,256]{3,2,1,0:T(8,128)S(1)}, f32[2,4,32,256]{3,2,1,0:T(8,128)S(1)}, u32[]{:S(2)}, u32[]{:S(2)}) collective-permute-start(f32[2,4,32,256]{3,2,1,0:T(8,128)S(1)} %get-tuple-element.124.hi), channel_id=1, source_target_pairs={{0,2},{8,10},{16,18},{24,26},{2,4},{10,12},{18,20},{26,28},{4,6},{... | collective-permute-start | bytes 786440 | tf_op jit(solution)/shard_map/ppermute | solution.py:39
  87.4 9.4 %collective-permute-start.35 = (f32[2,4,32,256]{3,2,1,0:T(8,128)S(1)}, f32[2,4,32,256]{3,2,1,0:T(8,128)S(1)}, u32[]{:S(2)}, u32[]{:S(2)}) collective-permute-start(f32[2,4,32,256]{3,2,1,0:T(8,128)S(1)} %get-tuple-element.123.lo), channel_id=1, source_target_pairs={{0,30},{8,6},{16,14},{24,22},{2,0},{10,8},{18,16},{26,24},{4,2},{1... | collective-permute-start | bytes 786440 | tf_op jit(solution)/shard_map/ppermute | solution.py:39
  100.3 3.7 %collective-permute-start.37 = (f32[2,4,16,256]{3,2,1,0:T(8,128)S(1)}, f32[2,4,16,256]{3,2,1,0:T(8,128)S(1)}, u32[]{:S(2)}, u32[]{:S(2)}) collective-permute-start(f32[2,4,16,256]{3,2,1,0:T(8,128)S(1)} %get-tuple-element.127), channel_id=1, source_target_pairs={{0,32},{8,40},{16,48},{24,56},{2,34},{10,42},{18,50},{26,58},{4,36... | collective-permute-start | bytes 393224 | tf_op jit(solution)/shard_map/ppermute | solution.py:39
  104.6 4.5 %collective-permute-start.38 = (f32[4,16,256]{2,1,0:T(8,128)S(1)}, f32[4,16,256]{2,1,0:T(8,128)S(1)}, u32[]{:S(2)}, u32[]{:S(2)}) collective-permute-start(f32[4,16,256]{2,1,0:T(8,128)S(1)} %get-tuple-element.129), channel_id=1, source_target_pairs={{0,64},{8,72},{16,80},{24,88},{2,66},{10,74},{18,82},{26,90},{4,68... | collective-permute-start | bytes 196616 | tf_op jit(solution)/shard_map/ppermute | solution.py:39
  105.5 5.6 %collective-permute-start.39 = (f32[4,16,256]{2,1,0:T(8,128)S(1)}, f32[4,16,256]{2,1,0:T(8,128)S(1)}, u32[]{:S(2)}, u32[]{:S(2)}) collective-permute-start(f32[4,16,256]{2,1,0:T(8,128)S(1)} %get-tuple-element.130), channel_id=1, source_target_pairs={{0,1},{8,9},{16,17},{24,25},{2,3},{10,11},{18,19},{26,27},{4,5},{1... | collective-permute-start | bytes 196616 | tf_op jit(solution)/shard_map/ppermute | solution.py:39
  107.6 4.0 %collective-permute-start.40 = (f32[4,16,256]{2,1,0:T(8,128)S(1)}, f32[4,16,256]{2,1,0:T(8,128)S(1)}, u32[]{:S(2)}, u32[]{:S(2)}) collective-permute-start(f32[4,16,256]{2,1,0:T(8,128)S(1)} %get-tuple-element.131), channel_id=1, source_target_pairs={{0,65},{8,73},{16,81},{24,89},{2,67},{10,75},{18,83},{26,91},{4,69... | collective-permute-start | bytes 196616 | tf_op jit(solution)/shard_map/ppermute | solution.py:39
  112.3 6.8 %collective-permute-start.41 = (f32[2,4,16,256]{3,2,1,0:T(8,128)S(1)}, f32[2,4,16,256]{3,2,1,0:T(8,128)S(1)}, u32[]{:S(2)}, u32[]{:S(2)}) collective-permute-start(f32[2,4,16,256]{3,2,1,0:T(8,128)S(1)} %get-tuple-element.133.last), channel_id=1, source_target_pairs={{0,30},{8,6},{16,14},{24,22},{2,0},{10,8},{18,16},{26,24},{4,2},{1... | collective-permute-start | bytes 393224 | tf_op jit(solution)/shard_map/ppermute | solution.py:39
  119.7 3.0 %collective-permute-start.42 = (f32[4,16,256]{2,1,0:T(8,128)S(1)}, f32[4,16,256]{2,1,0:T(8,128)S(1)}, u32[]{:S(2)}, u32[]{:S(2)}) collective-permute-start(f32[4,16,256]{2,1,0:T(8,128)S(1)} %get-tuple-element.136), channel_id=1, source_target_pairs={{0,32},{8,40},{16,48},{24,56},{2,34},{10,42},{18,50},{26,58},{4,36... | collective-permute-start | bytes 196616 | tf_op jit(solution)/shard_map/ppermute | solution.py:39
